TPU v7x, 512 devices: a whole 4x4x16 slice. The times are simulated.
512 devices in a mesh: box: 64 (over x, z_hi, y, core), freq: 8 (over z_lo).
Axes of the slice: x: 4, y: 4, z: 16 (z_hi: 2, z_lo: 8; z = z_hi * 8 + z_lo), core: 2. Of those that a mesh axis runs over, the one named last changes fastest.
Arguments:
- spectra_fine: bfloat16 [4096, 2, 8, 1024], P(('box', 'freq')), may hold values from -6 to 6
- spectra_coarse: bfloat16 [512, 2, 8, 1024], P(('box', 'freq')), may hold values from -6 to 6
- kernel_table: bfloat16 [26, 2, 8, 8, 1024], P(None, None, None, None, 'freq'), may hold values from -0.3125 to 0.3125
- lists_fine: int32 [4096, 26], P('box'), may hold values from -1 to 4095, as said below
- lists_coarse: int32 [512, 26], P('box'), may hold values from -1 to 511, as said below
- live_counts: int32 [64, 2], P('box'), may hold values from 4 to 64, as said below
Outputs:
- potentials_fine: bfloat16 [4096, 2, 8, 1024], P('box', None, None, 'freq')
- potentials_coarse: bfloat16 [512, 2, 8, 1024], P('box', None, None, 'freq')
Inputs may be any that keep to these rules, and one draw needn't show every extreme that they name: `lists_fine`: each entry is -1 or a group whose Morton index differs from the target's by at most 16; that distance is reached. `lists_coarse`: each entry is -1 or a group whose Morton index differs from the target's by at most 2; that distance is reached. `live_counts`: column 0 lies in 32 to 64, column 1 in 4 to 8; each column reaches its largest value on some index.
All inputs are finite; a program needn't handle non-finite values.
Results may differ from a plain program's by a relative error of at most 0.007.
Values may be sent and summed in bfloat16 or wider, within the bound.
A program may use at most 64 MiB of HBM per device.

v0:
```python
import jax
import jax.numpy as jnp
from jax import lax
from jax.sharding import PartitionSpec as P

RIM_FINE = 16
RIM_COARSE = 2


def padded_2(block, sides, width):
    for axis, dim in sides:
        count = lax.axis_size(axis)
        forward = [(i, i + 1) for i in range(count - 1)]
        backward = [(target, source) for source, target in forward]
        low = lax.ppermute(
            lax.slice_in_dim(block, block.shape[dim] - width, None, axis=dim), axis, forward
        )
        high = lax.ppermute(lax.slice_in_dim(block, 0, width, axis=dim), axis, backward)
        block = jnp.concatenate([low, block, high], axis=dim)
    return block


def passed_along(value, axis, steps):
    count = lax.axis_size(axis)
    leading, last = (max(0, -steps), min(count, count - steps))
    return lax.ppermute(value, axis, [(source, source + steps) for source in range(leading, last)])


def contract(padded, source_index, kernel_table):
    target_rows = source_index.shape[0]
    width = kernel_table.shape[-1]
    totals = jnp.zeros((target_rows, 2, 8, width), jnp.float32)
    for first_slot in range(0, source_index.shape[1], 8):
        picked = jnp.take(padded, source_index[:, first_slot : first_slot + 8], axis=0)
        kernel_block = kernel_table[first_slot : first_slot + 8]
        picked_real = picked[:, :, 0][:, :, None].astype(jnp.float32)
        picked_imag = picked[:, :, 1][:, :, None].astype(jnp.float32)
        kernel_real = kernel_block[:, 0][None].astype(jnp.float32)
        kernel_imag = kernel_block[:, 1][None].astype(jnp.float32)
        real_part = jnp.sum(picked_real * kernel_real - picked_imag * kernel_imag, axis=(1, 3))
        imag_part = jnp.sum(picked_imag * kernel_real + picked_real * kernel_imag, axis=(1, 3))
        totals = totals + jnp.stack([real_part, imag_part], 1)
    return totals


def alive_rows(group_count, live_count):
    places = jnp.arange(group_count, dtype=jnp.int32)
    lower_live = live_count // 2
    return (places < lower_live) | (places >= group_count - (live_count - lower_live))


def mask_rows(values, alive_mask):
    return jnp.where(alive_mask[:, None, None, None], values, jnp.zeros_like(values))


def append_zero(values):
    return jnp.concatenate([values, jnp.zeros((1,) + values.shape[1:], values.dtype)], 0)


def per_device(spectra_fine, spectra_coarse, kernel_table, lists_fine, lists_coarse, live_counts):
    owned_fine, owned_coarse = (
        lax.all_to_all(spectra_fine, "freq", split_axis=3, concat_axis=0, tiled=True),
        lax.all_to_all(spectra_coarse, "freq", split_axis=3, concat_axis=0, tiled=True),
    )
    position = lax.axis_index("box")
    rows_fine = owned_fine.shape[0]
    rows_coarse = owned_coarse.shape[0]
    alive_fine = alive_rows(rows_fine, live_counts[0, 0])
    alive_coarse = alive_rows(rows_coarse, live_counts[0, 1])
    masked_fine = mask_rows(owned_fine, alive_fine)
    masked_coarse = mask_rows(owned_coarse, alive_coarse)
    extended_fine = padded_2(lists_fine, (("box", 0),), RIM_FINE)
    extended_coarse = padded_2(lists_coarse, (("box", 0),), RIM_COARSE)

    def spread(masked, extended, group_count, level_scale):
        local_index = extended - position * group_count
        usable = (extended >= 0) & (local_index >= 0) & (local_index < group_count)
        source_index = jnp.where(usable, local_index, group_count)
        return level_scale * contract(append_zero(masked), source_index, kernel_table)

    partial_fine = spread(masked_fine, extended_fine, rows_fine, 1.0)
    partial_coarse = spread(masked_coarse, extended_coarse, rows_coarse, 0.5)
    from_above = (
        passed_along(partial_fine[:RIM_FINE].astype(jnp.bfloat16), "box", -1).astype(jnp.float32),
        passed_along(partial_coarse[:RIM_COARSE].astype(jnp.bfloat16), "box", -1).astype(
            jnp.float32
        ),
    )
    from_below = (
        passed_along(partial_fine[RIM_FINE + rows_fine :].astype(jnp.bfloat16), "box", 1).astype(
            jnp.float32
        ),
        passed_along(
            partial_coarse[RIM_COARSE + rows_coarse :].astype(jnp.bfloat16), "box", 1
        ).astype(jnp.float32),
    )
    result_fine = partial_fine[RIM_FINE : RIM_FINE + rows_fine]
    result_fine = (
        result_fine.at[:RIM_FINE].add(from_below[0]).at[rows_fine - RIM_FINE :].add(from_above[0])
    )
    result_coarse = partial_coarse[RIM_COARSE : RIM_COARSE + rows_coarse]
    result_coarse = (
        result_coarse.at[:RIM_COARSE]
        .add(from_below[1])
        .at[rows_coarse - RIM_COARSE :]
        .add(from_above[1])
    )
    potentials_fine = mask_rows(result_fine, alive_fine).astype(jnp.bfloat16)
    potentials_coarse = mask_rows(result_coarse, alive_coarse).astype(jnp.bfloat16)
    return (potentials_fine, potentials_coarse)


def solution(mesh):
    return jax.shard_map(
        per_device,
        mesh=mesh,
        in_specs=(
            P(("box", "freq"), None, None, None),
            P(("box", "freq"), None, None, None),
            P(None, None, None, None, "freq"),
            P("box", None),
            P("box", None),
            P("box", None),
        ),
        out_specs=(P("box", None, None, "freq"), P("box", None, None, "freq")),
        check_vma=False,
    )
```

profile of v0, /device:TPU:475, one launch (start us, length us, event | category | flops | bytes accessed | tf_op | source)
XLA Modules:
  0.0 243.7 jit_solution(8473077162758704728)
XLA Ops:
  0.6 1.1 copy.77
  1.8 1.1 reshape.376
  2.9 8.9 %all-to-all-start.1 = ((bf16[8,2,1024]{2,1,0:T(2,128)(2,1)}), bf16[8,2,1024]{2,1,0:T(2,128)(2,1)S(1)}, u32[]{:S(2)}, u32[]{:S(2)}) async-start(bf16[8,2,1024]{2,1,0:T(2,128)(2,1)} %reshape.376), calls=%async_computation.1 | async-start | bytes 65536 | tf_op jit(solution)/shard_map/all_to_all | solution.py:63
  11.8 0.8 fusion.32
  12.6 7.8 %collective-permute-start.4 = (s32[2,26]{1,0:T(2,128)S(1)}, s32[2,26]{1,0:T(2,128)S(1)}, u32[]{:S(2)}, u32[]{:S(2)}) collective-permute-start(s32[2,26]{1,0:T(2,128)S(1)} %get-tuple-element.118), channel_id=1, source_target_pairs={{0,8},{8,16},{16,24},{24,32},{32,40},{40,48},{48,56},{56,64},{64,7... | collective-permute-start | bytes 632 | tf_op jit(solution)/shard_map/ppermute | solution.py:15
  20.3 1.9 collective-permute-start.5
  22.2 0.9 fusion.31
  23.1 15.4 %collective-permute-start = (s32[16,26]{0,1:T(8,128)S(1)}, s32[16,26]{0,1:T(8,128)S(1)}, u32[]{:S(2)}, u32[]{:S(2)}) collective-permute-start(s32[16,26]{0,1:T(8,128)S(1)} %get-tuple-element.110), channel_id=1, source_target_pairs={{0,8},{8,16},{16,24},{24,32},{32,40},{40,48},{48,56},{56,64},{64,7... | collective-permute-start | bytes 5000 | tf_op jit(solution)/shard_map/ppermute | solution.py:15
  38.5 1.9 collective-permute-start.1
  40.4 1.3 fusion.33
  44.3 1.4 bitcast_convert_fusion.5
  45.8 1.5 bitcast_convert_fusion.7
  51.9 4.7 %copy.68 = bf16[8,2,8,1024]{2,0,1,3:T(8,128)(2,1)} copy(bf16[8,2,8,1024]{3,2,1,0:T(8,128)(2,1)S(1)} %copy-done.15) | data formatting | bytes 524288 | tf_op args[0]
  56.6 6.4 %reshape.374 = bf16[8,2,8192]{2,1,0:T(2,128)(2,1)} reshape(bf16[1024,2,8,8]{3,2,1,0:T(8,128)(2,1)} %bitcast.144) | data formatting | bytes 524288
  65.3 9.4 %all-to-all-start = ((bf16[8,2,8192]{2,1,0:T(2,128)(2,1)}), bf16[8,2,8192]{2,1,0:T(2,128)(2,1)S(1)}, u32[]{:S(2)}, u32[]{:S(2)}) async-start(bf16[8,2,8192]{2,1,0:T(2,128)(2,1)} %reshape.374), calls=%async_computation | async-start | bytes 524288 | tf_op jit(solution)/shard_map/all_to_all | solution.py:62
  77.5 1.0 fusion.11
  79.4 1.2 gather_fusion.1
  80.6 1.0 broadcast_select_fusion.8
  81.7 1.0 subtract_reduce_fusion.6
  82.7 3.3 %subtract_reduce_fusion.4 = (f32[12,8,128]{2,1,0:T(8,128)S(1)}, f32[12,8,128]{2,1,0:T(8,128)S(1)}, f32[12,8,128]{2,1,0:T(8,128)S(1)}, f32[12,8,128]{2,1,0:T(8,128)S(1)}) fusion(f32[8,8,8,128]{3,2,1,0:T(8,128)S(1)} %get-tuple-element.83, f32[12,8,8,128]{3,2,1,0:T(8,128)} %get-tuple-element.97, f32[8,8,8,128]{3,2,1,0:T(8,128)S(1)} %get-tuple-element.84, ...), kind=kLoop, calls=%fused_computation.17 | loop fusion | flops 12533760 | bytes 2818048 | tf_op jit(solution)/shard_map/reduce_sum | solution.py:40
  86.5 15.9 %collective-permute-start.6 = (bf16[2,2,8,128]{3,2,1,0:T(8,128)(2,1)S(1)}, bf16[2,2,8,128]{3,2,1,0:T(8,128)(2,1)S(1)}, u32[]{:S(2)}, u32[]{:S(2)}) collective-permute-start(bf16[2,2,8,128]{3,2,1,0:T(8,128)(2,1)S(1)} %get-tuple-element.103), channel_id=1, source_target_pairs={{0,8},{8,16},{16,24},{24,32},{32,40},{40,48},{48,56},{56,64},{64,7... | collective-permute-start | bytes 24584 | tf_op jit(solution)/shard_map/ppermute | solution.py:26
  102.4 0.7 copy.67
  103.1 0.7 copy.71
  104.0 0.8 copy.75
  105.4 2.1 collective-permute-start.7
  108.1 14.1 %collective-permute-done.7 = bf16[2,2,8,128]{3,2,1,0:T(8,128)(2,1)S(1)} collective-permute-done((bf16[2,2,8,128]{3,2,1,0:T(8,128)(2,1)S(1)}, bf16[2,2,8,128]{3,2,1,0:T(8,128)(2,1)S(1)}, u32[]{:S(2)}, u32[]{:S(2)}) %collective-permute-start.7) | collective-permute-done | bytes 8224 | tf_op jit(solution)/shard_map/ppermute | solution.py:26
  122.2 1.3 fusion.23
  123.5 5.9 %reshape.375 = bf16[1024,2,8,8]{3,2,1,0:T(8,128)(2,1)} reshape(bf16[8,2,8192]{2,1,0:T(2,128)(2,1)S(1)} %all-to-all-done) | data formatting | bytes 524288
  129.5 3.9 %copy.69 = bf16[8,2,8,8,128]{4,2,0,3,1:T(8,128)(2,1)S(1)} copy(bf16[8,2,8,8,128]{2,0,1,4,3:T(8,128)(2,1)} %bitcast.143) | data formatting | bytes 524288 | tf_op jit(solution)/shard_map/all_to_all | solution.py:62
  133.6 2.8 %gather_fusion.2 = bf16[768,2,8,128]{3,2,1,0:T(8,128)(2,1)S(1)} fusion(bf16[65,2,8,128]{3,2,0,1:T(8,128)(2,1)S(1)} %concatenate.20, s32[1024]{0:T(1024)S(1)} %pad_clamp_fusion.7), kind=kCustom, calls=%fused_computation.clone | custom fusion | bytes 6294528 | tf_op jit(solution)/shard_map/jit(_take)/gather | solution.py:34
  136.4 1.1 broadcast_select_fusion.2
  137.6 3.8 %fusion.5 = (f32[96,8,8,128]{3,2,1,0:T(8,128)}, f32[96,8,8,128]{3,2,1,0:T(8,128)}) fusion(bf16[96,8,2,8,128]{4,3,2,1,0:T(8,128)(2,1)S(1)} %broadcast_select_fusion.2), kind=kLoop, calls=%fused_computation.36 | loop fusion | flops 1572864 | bytes 9437184 | tf_op jit(solution)/shard_map/mul | solution.py:40
  141.3 2.8 %gather_fusion.3 = bf16[768,2,8,128]{3,2,1,0:T(8,128)(2,1)S(1)} fusion(bf16[65,2,8,128]{3,2,0,1:T(8,128)(2,1)S(1)} %concatenate.20, s32[1024]{0:T(1024)S(1)} %pad_clamp_fusion.6), kind=kCustom, calls=%fused_computation.2.clone | custom fusion | bytes 6294528 | tf_op jit(solution)/shard_map/jit(_take)/gather | solution.py:34
  144.2 1.1 broadcast_select_fusion.1
  145.3 3.7 %fusion.3 = (f32[96,8,8,128]{3,2,1,0:T(8,128)}, f32[96,8,8,128]{3,2,1,0:T(8,128)}) fusion(bf16[96,8,2,8,128]{4,3,2,1,0:T(8,128)(2,1)S(1)} %broadcast_select_fusion.1), kind=kLoop, calls=%fused_computation.32 | loop fusion | flops 1572864 | bytes 9437184 | tf_op jit(solution)/shard_map/mul | solution.py:40
  149.0 2.8 %gather_fusion.4 = bf16[768,2,8,128]{3,2,1,0:T(8,128)(2,1)S(1)} fusion(bf16[65,2,8,128]{3,2,0,1:T(8,128)(2,1)S(1)} %concatenate.20, s32[1024]{0:T(1024)S(1)} %pad_clamp_fusion.5), kind=kCustom, calls=%fused_computation.3.clone | custom fusion | bytes 6294528 | tf_op jit(solution)/shard_map/jit(_take)/gather | solution.py:34
  151.9 1.1 broadcast_select_fusion
  153.0 3.7 %fusion.1 = (f32[96,8,8,128]{3,2,1,0:T(8,128)}, f32[96,8,8,128]{3,2,1,0:T(8,128)}) fusion(bf16[96,8,2,8,128]{4,3,2,1,0:T(8,128)(2,1)S(1)} %broadcast_select_fusion), kind=kLoop, calls=%fused_computation.28 | loop fusion | flops 1572864 | bytes 9437184 | tf_op jit(solution)/shard_map/mul | solution.py:40
  156.7 1.7 gather_fusion
  158.5 1.5 broadcast_select_fusion.3
  160.1 13.8 %subtract_reduce_fusion.2 = (f32[96,8,128]{2,1,0:T(8,128)}, f32[96,8,128]{2,1,0:T(8,128)}) fusion(f32[8,8,8,128]{3,2,1,0:T(8,128)S(1)} %copy-done.6, f32[96,8,8,128]{3,2,1,0:T(8,128)} %get-tuple-element.77, f32[8,8,8,128]{3,2,1,0:T(8,128)S(1)} %copy-done.4, f32[96,8,8,128]{3,2,1,0:T(8,128)S(1)} %copy-done), kind=kLoop, calls=%fused_computation.13 | loop fusion | flops 50135040 | bytes 7602176 | tf_op jit(solution)/shard_map/reduce_sum | solution.py:40
  174.0 4.1 %subtract_reduce_fusion.3 = (f32[96,8,128]{2,1,0:T(8,128)S(1)}, f32[96,8,128]{2,1,0:T(8,128)S(1)}) fusion(f32[2,8,8,128]{3,2,1,0:T(8,128)S(1)} %copy-done.14, f32[96,2,8,128]{3,2,1,0:T(8,128)S(1)} %get-tuple-element.91, f32[2,8,8,128]{3,2,1,0:T(8,128)S(1)} %get-tuple-element.88, f32[96,2,8,128]{3,2,1,0:T(8,128)S(1)} %get-tuple-element.90), kind=kLoop, calls=%fused_computation.15 | loop fusion | flops 12386304 | bytes 2490368 | tf_op jit(solution)/shard_map/reduce_sum | solution.py:40
  178.2 42.2 %subtract_reduce_fusion = (f32[96,8,128]{2,1,0:T(8,128)S(1)}, f32[96,8,128]{2,1,0:T(8,128)S(1)}, f32[96,8,128]{2,1,0:T(8,128)S(1)}, f32[96,8,128]{2,1,0:T(8,128)S(1)}) fusion(f32[8,8,8,128]{3,2,1,0:T(8,128)} %copy-done.7, f32[96,8,8,128]{3,2,1,0:T(8,128)} %get-tuple-element.81, f32[8,8,8,128]{3,2,1,0:T(8,128)} %copy-done.8, ...), kind=kLoop, calls=%fused_computation.9 | loop fusion | flops 100270080 | bytes 15204352 | tf_op jit(solution)/shard_map/reduce_sum | solution.py:40
  220.6 1.9 collective-permute-start.2
  222.5 1.5 select_convert_fusion.1
  224.1 2.4 collective-permute-start.3
  226.6 16.3 %collective-permute-done.3 = bf16[16,2,8,128]{3,2,0,1:T(8,128)(2,1)S(1)} collective-permute-done((bf16[16,2,8,128]{3,2,0,1:T(8,128)(2,1)S(1)}, bf16[16,2,8,128]{3,2,0,1:T(8,128)(2,1)S(1)}, u32[]{:S(2)}, u32[]{:S(2)}) %collective-permute-start.3) | collective-permute-done | bytes 65568 | tf_op jit(solution)/shard_map/ppermute | solution.py:26
  243.0 0.7 copy.80
  (114 shorter events, 8.9 us)
Async XLA Ops:
  0.6 51.2 %copy-start.15 = (bf16[8,2,8,1024]{3,2,1,0:T(8,128)(2,1)S(1)}, bf16[8,2,8,1024]{3,2,1,0:T(8,128)(2,1)}, u32[]{:S(2)}) copy-start(bf16[8,2,8,1024]{3,2,1,0:T(8,128)(2,1)} %param.18) | copy-start | bytes 786436
  2.9 62.4 %all-to-all-start.1 = ((bf16[8,2,1024]{2,1,0:T(2,128)(2,1)}), bf16[8,2,1024]{2,1,0:T(2,128)(2,1)S(1)}, u32[]{:S(2)}, u32[]{:S(2)}) async-start(bf16[8,2,1024]{2,1,0:T(2,128)(2,1)} %reshape.376), calls=%async_computation.1 | async-start | bytes 65536 | tf_op jit(solution)/shard_map/all_to_all | solution.py:63
  12.6 50.4 %collective-permute-start.4 = (s32[2,26]{1,0:T(2,128)S(1)}, s32[2,26]{1,0:T(2,128)S(1)}, u32[]{:S(2)}, u32[]{:S(2)}) collective-permute-start(s32[2,26]{1,0:T(2,128)S(1)} %get-tuple-element.118), channel_id=1, source_target_pairs={{0,8},{8,16},{16,24},{24,32},{32,40},{40,48},{48,56},{56,64},{64,7... | collective-permute-start | bytes 632 | tf_op jit(solution)/shard_map/ppermute | solution.py:15
  20.3 42.7 %collective-permute-start.5 = (s32[2,26]{1,0:T(2,128)S(1)}, s32[2,26]{1,0:T(2,128)S(1)}, u32[]{:S(2)}, u32[]{:S(2)}) collective-permute-start(s32[2,26]{1,0:T(2,128)S(1)} %get-tuple-element.119), channel_id=1, source_target_pairs={{8,0},{16,8},{24,16},{32,24},{40,32},{48,40},{56,48},{64,56},{72,6... | collective-permute-start | bytes 632 | tf_op jit(solution)/shard_map/ppermute | solution.py:18
  23.1 40.6 %collective-permute-start = (s32[16,26]{0,1:T(8,128)S(1)}, s32[16,26]{0,1:T(8,128)S(1)}, u32[]{:S(2)}, u32[]{:S(2)}) collective-permute-start(s32[16,26]{0,1:T(8,128)S(1)} %get-tuple-element.110), channel_id=1, source_target_pairs={{0,8},{8,16},{16,24},{24,32},{32,40},{40,48},{48,56},{56,64},{64,7... | collective-permute-start | bytes 5000 | tf_op jit(solution)/shard_map/ppermute | solution.py:15
  38.5 25.3 %collective-permute-start.1 = (s32[16,26]{0,1:T(8,128)S(1)}, s32[16,26]{0,1:T(8,128)S(1)}, u32[]{:S(2)}, u32[]{:S(2)}) collective-permute-start(s32[16,26]{0,1:T(8,128)S(1)} %get-tuple-element.111), channel_id=1, source_target_pairs={{8,0},{16,8},{24,16},{32,24},{40,32},{48,40},{56,48},{64,56},{72,6... | collective-permute-start | bytes 5000 | tf_op jit(solution)/shard_map/ppermute | solution.py:18
  45.7 36.0 %copy-start.3 = (f32[8,8,8,128]{3,2,1,0:T(8,128)}, f32[8,8,8,128]{3,2,1,0:T(8,128)S(1)}, u32[]{:S(2)}) copy-start(f32[8,8,8,128]{3,2,1,0:T(8,128)S(1)} %get-tuple-element.82) | copy-start | bytes 786436
  45.7 36.0 %copy-start.5 = (f32[8,8,8,128]{3,2,1,0:T(8,128)}, f32[8,8,8,128]{3,2,1,0:T(8,128)S(1)}, u32[]{:S(2)}) copy-start(f32[8,8,8,128]{3,2,1,0:T(8,128)S(1)} %get-tuple-element.87) | copy-start | bytes 786436
  45.7 37.0 %copy-start.7 = (f32[8,8,8,128]{3,2,1,0:T(8,128)}, f32[8,8,8,128]{3,2,1,0:T(8,128)S(1)}, u32[]{:S(2)}) copy-start(f32[8,8,8,128]{3,2,1,0:T(8,128)S(1)} %get-tuple-element.83) | copy-start | bytes 786436
  45.7 37.0 %copy-start.8 = (f32[8,8,8,128]{3,2,1,0:T(8,128)}, f32[8,8,8,128]{3,2,1,0:T(8,128)S(1)}, u32[]{:S(2)}) copy-start(f32[8,8,8,128]{3,2,1,0:T(8,128)S(1)} %get-tuple-element.84) | copy-start | bytes 786436
  45.7 37.0 %copy-start.9 = (f32[8,8,8,128]{3,2,1,0:T(8,128)}, f32[8,8,8,128]{3,2,1,0:T(8,128)S(1)}, u32[]{:S(2)}) copy-start(f32[8,8,8,128]{3,2,1,0:T(8,128)S(1)} %get-tuple-element.85) | copy-start | bytes 786436
  45.8 37.0 %copy-start.10 = (f32[8,8,8,128]{3,2,1,0:T(8,128)}, f32[8,8,8,128]{3,2,1,0:T(8,128)S(1)}, u32[]{:S(2)}) copy-start(f32[8,8,8,128]{3,2,1,0:T(8,128)S(1)} %get-tuple-element.86) | copy-start | bytes 786436
  50.6 24.9 %copy-start.20 = (pred[8]{0:T(512)(128)(4,1)}, pred[8]{0:T(512)(128)(4,1)S(1)}, u32[]{:S(2)}) copy-start(pred[8]{0:T(512)(128)(4,1)S(1)} %compare_or_fusion) | copy-start | bytes 28
  56.6 6.5 %copy-start.19 = (s32[8,26]{1,0:T(8,128)S(1)}, s32[8,26]{1,0:T(8,128)}, u32[]{:S(2)}) copy-start(s32[8,26]{1,0:T(8,128)} %param.22) | copy-start | bytes 2500
  56.6 7.2 %copy-start.16 = (s32[64,26]{0,1:T(8,128)S(1)}, s32[64,26]{0,1:T(8,128)}, u32[]{:S(2)}) copy-start(s32[64,26]{0,1:T(8,128)} %param.21) | copy-start | bytes 19972
  65.3 58.2 %all-to-all-start = ((bf16[8,2,8192]{2,1,0:T(2,128)(2,1)}), bf16[8,2,8192]{2,1,0:T(2,128)(2,1)S(1)}, u32[]{:S(2)}, u32[]{:S(2)}) async-start(bf16[8,2,8192]{2,1,0:T(2,128)(2,1)} %reshape.374), calls=%async_computation | async-start | bytes 524288 | tf_op jit(solution)/shard_map/all_to_all | solution.py:62
  80.6 5.4 %copy-start.13 = (f32[2,8,8,128]{3,2,1,0:T(8,128)S(1)}, f32[2,8,8,128]{3,2,1,0:T(8,128)}, u32[]{:S(2)}) copy-start(f32[2,8,8,128]{3,2,1,0:T(8,128)} %get-tuple-element.89) | copy-start | bytes 196612
  86.5 21.0 %collective-permute-start.6 = (bf16[2,2,8,128]{3,2,1,0:T(8,128)(2,1)S(1)}, bf16[2,2,8,128]{3,2,1,0:T(8,128)(2,1)S(1)}, u32[]{:S(2)}, u32[]{:S(2)}) collective-permute-start(bf16[2,2,8,128]{3,2,1,0:T(8,128)(2,1)S(1)} %get-tuple-element.103), channel_id=1, source_target_pairs={{0,8},{8,16},{16,24},{24,32},{32,40},{40,48},{48,56},{56,64},{64,7... | collective-permute-start | bytes 24584 | tf_op jit(solution)/shard_map/ppermute | solution.py:26
  105.4 16.9 %collective-permute-start.7 = (bf16[2,2,8,128]{3,2,1,0:T(8,128)(2,1)S(1)}, bf16[2,2,8,128]{3,2,1,0:T(8,128)(2,1)S(1)}, u32[]{:S(2)}, u32[]{:S(2)}) collective-permute-start(bf16[2,2,8,128]{3,2,1,0:T(8,128)(2,1)S(1)} %get-tuple-element.102), channel_id=1, source_target_pairs={{8,0},{16,8},{24,16},{32,24},{40,32},{48,40},{56,48},{64,56},{72,6... | collective-permute-start | bytes 24584 | tf_op jit(solution)/shard_map/ppermute | solution.py:26
  129.5 3.9 %copy-start.22 = (pred[64]{0:T(512)(128)(4,1)S(1)}, pred[64]{0:T(512)(128)(4,1)}, u32[]{:S(2)}) copy-start(pred[64]{0:T(512)(128)(4,1)} %compare_or_fusion.1) | copy-start | bytes 196
  133.6 2.8 %copy-start.18 = (pred[96,8]{1,0:T(8,128)(4,1)S(1)}, pred[96,8]{1,0:T(8,128)(4,1)}, u32[]{:S(2)}) copy-start(pred[96,8]{1,0:T(8,128)(4,1)} %copy.67) | copy-start | bytes 2308
  141.3 2.8 %copy-start.17 = (pred[96,8]{1,0:T(8,128)(4,1)S(1)}, pred[96,8]{1,0:T(8,128)(4,1)}, u32[]{:S(2)}) copy-start(pred[96,8]{1,0:T(8,128)(4,1)} %copy.71) | copy-start | bytes 2308
  156.7 3.3 %copy-start = (f32[96,8,8,128]{3,2,1,0:T(8,128)S(1)}, f32[96,8,8,128]{3,2,1,0:T(8,128)}, u32[]{:S(2)}) copy-start(f32[96,8,8,128]{3,2,1,0:T(8,128)} %get-tuple-element.76) | copy-start | bytes 9437188
  158.5 1.6 copy-start.4
  158.5 1.6 copy-start.6
  160.1 13.9 %copy-start.14 = (f32[2,8,8,128]{3,2,1,0:T(8,128)S(1)}, f32[2,8,8,128]{3,2,1,0:T(8,128)}, u32[]{:S(2)}) copy-start(f32[2,8,8,128]{3,2,1,0:T(8,128)} %get-tuple-element.89) | copy-start | bytes 196612
  160.1 18.0 %copy-start.1 = (f32[96,8,8,128]{3,2,1,0:T(8,128)S(1)}, f32[96,8,8,128]{3,2,1,0:T(8,128)}, u32[]{:S(2)}) copy-start(f32[96,8,8,128]{3,2,1,0:T(8,128)} %get-tuple-element.78) | copy-start | bytes 9437188
  160.1 18.0 %copy-start.2 = (f32[96,8,8,128]{3,2,1,0:T(8,128)S(1)}, f32[96,8,8,128]{3,2,1,0:T(8,128)}, u32[]{:S(2)}) copy-start(f32[96,8,8,128]{3,2,1,0:T(8,128)} %get-tuple-element.79) | copy-start | bytes 9437188
  178.1 42.3 %copy-start.11 = (f32[96,8,128]{2,1,0:T(8,128)S(1)}, f32[96,8,128]{2,1,0:T(8,128)}, u32[]{:S(2)}) copy-start(f32[96,8,128]{2,1,0:T(8,128)} %get-tuple-element.60) | copy-start | bytes 1179652
  178.2 42.3 %copy-start.12 = (f32[96,8,128]{2,1,0:T(8,128)S(1)}, f32[96,8,128]{2,1,0:T(8,128)}, u32[]{:S(2)}) copy-start(f32[96,8,128]{2,1,0:T(8,128)} %get-tuple-element.61) | copy-start | bytes 1179652
  220.4 2.1 copy-start.21
  220.6 5.9 %collective-permute-start.2 = (bf16[16,2,8,128]{3,2,0,1:T(8,128)(2,1)S(1)}, bf16[16,2,8,128]{3,2,0,1:T(8,128)(2,1)S(1)}, u32[]{:S(2)}, u32[]{:S(2)}) collective-permute-start(bf16[16,2,8,128]{3,2,0,1:T(8,128)(2,1)S(1)} %get-tuple-element.99), channel_id=1, source_target_pairs={{0,8},{8,16},{16,24},{24,32},{32,40},{40,48},{48,56},{56,64},{64,7... | collective-permute-start | bytes 196616 | tf_op jit(solution)/shard_map/ppermute | solution.py:26
  224.1 18.7 %collective-permute-start.3 = (bf16[16,2,8,128]{3,2,0,1:T(8,128)(2,1)S(1)}, bf16[16,2,8,128]{3,2,0,1:T(8,128)(2,1)S(1)}, u32[]{:S(2)}, u32[]{:S(2)}) collective-permute-start(bf16[16,2,8,128]{3,2,0,1:T(8,128)(2,1)S(1)} %get-tuple-element.98), channel_id=1, source_target_pairs={{8,0},{16,8},{24,16},{32,24},{40,32},{48,40},{56,48},{64,56},{72,6... | collective-permute-start | bytes 196616 | tf_op jit(solution)/shard_map/ppermute | solution.py:26
where the time goes:
time: 245 us; the launch traced here: 244 us
  other arithmetic  92.3 us (38%)
  starting transfers between devices  67.5 us (28%)
  local copies, waits for them, and re-layouts  45.4 us (19%)
  waiting for transfers between devices  30.4 us (12%)
  between operations  8.08 us (3%)
    reduce_sum x6, other arithmetic, contract(): jnp.sum(picked_real * kernel_real - picked_imag * kernel_imag, axis=(1, 3))  64.9 us
    ppermute x4, waiting for transfers between devices, passed_along(): lax.ppermute(value, axis, [(source, source + steps) for source in range(l...  30.4 us
    ppermute x2, starting transfers between devices, padded_2(): lax.ppermute(lax.slice_in_dim(block, block.shape[dim] - width, None, axis...  23.1 us
    ppermute x4, starting transfers between devices, passed_along(): lax.ppermute(value, axis, [(source, source + steps) for source in range(l...  22.3 us
    unnamed x53, local copies, waits for them, and re-layouts  20.8 us
    gather x8, local copies, waits for them, and re-layouts, contract(): jnp.take(padded, source_index[:, first_slot:first_slot + 8], axis=0)  13.4 us
    mul x8, other arithmetic, contract(): picked_real * kernel_real - picked_imag * kernel_imag  12.5 us
    all_to_all x1, starting transfers between devices, per_device(): lax.all_to_all(spectra_fine, 'freq', split_axis=3, concat_axis=0, tiled=T...  9.36 us
  transfers between devices with their start and end apart: 10, of which 2 were waited for; matrix products, arithmetic and copies ran while one was open for 15% of the time, Pallas kernels for 0%

commit v1 on v0

v1 whole, which is shorter than its diff:
```python
import functools

import jax
import jax.numpy as jnp
from jax import lax
from jax.experimental import pallas as pl
from jax.experimental.pallas import tpu as pltpu
from jax.sharding import PartitionSpec as P

RIM_FINE = 16
RIM_COARSE = 2
LANES = 128
BAND = 16
BANDS = LANES // BAND
PAIRS = BANDS // 2
WIDE = 2 * 8 * BAND


def swap_blocks(planes):
    block = lax.broadcasted_iota(jnp.int32, planes[0].shape, 1) // BAND
    planes = list(planes)
    for step in (4, 2, 1):
        upper = (block & step) != 0
        for p in range(8):
            if p & step == 0:
                first, second = planes[p], planes[p + step]
                planes[p] = jnp.where(upper, pltpu.roll(second, BAND * step, 1), first)
                planes[p + step] = jnp.where(upper, second, pltpu.roll(first, LANES - BAND * step, 1))
    return planes


def interleave():
    row = lax.broadcasted_iota(jnp.int32, (WIDE, WIDE), 0)
    lane = lax.broadcasted_iota(jnp.int32, (WIDE, WIDE), 1)
    hit = (row // BAND == lane % BAND) & (row % BAND == lane // BAND)
    return jnp.where(hit, 1.0, 0.0).astype(jnp.bfloat16)


def by_band(parts, permutation):
    planes = []
    for part in parts:
        turned = jnp.swapaxes(part, 0, 1)
        planes.append(swap_blocks([turned[i] for i in range(8)]))
    stacked = jnp.concatenate(
        [jnp.concatenate([planes[0][g], planes[1][g]], axis=1) for g in range(BANDS)], axis=0
    ).astype(jnp.bfloat16)
    return jnp.dot(stacked, permutation, preferred_element_type=jnp.float32).astype(jnp.bfloat16)


def alive(place, count, live):
    lower = live // 2
    return (place < lower) | (place >= count - (live - lower))


def kernel(
    n_box,
    n_freq,
    live_ref,
    fine_ref,
    coarse_ref,
    table_ref,
    lists_fine_ref,
    lists_coarse_ref,
    out_fine_ref,
    out_coarse_ref,
    outbox,
    outbox_coarse,
    held,
    held_coarse,
    picks,
    weights,
    gathered,
    sums,
    send_sem,
    recv_sem,
    rim_send,
    rim_recv,
    coarse_send,
    coarse_recv,
    coarse_rim_send,
    coarse_rim_recv,
):
    box = lax.axis_index("box")
    col = lax.axis_index("freq")
    above = lax.rem(box + 1, n_box)
    below = lax.rem(box + n_box - 1, n_box)
    slots = table_ref.shape[0]
    groups = lists_fine_ref.shape[0]
    coarse_groups = lists_coarse_ref.shape[0]
    own = fine_ref.shape[0]
    rows = groups + 16
    live_fine = live_ref[0, 0]
    live_coarse = live_ref[0, 1]
    order = (4, 3, 5, 2, 6, 1, 7)

    barrier = pltpu.get_barrier_semaphore()
    for step in range(1, n_freq):
        pl.semaphore_signal(barrier, inc=1, device_id={"freq": lax.rem(col + step, n_freq)})
    for other in (above, below):
        pl.semaphore_signal(barrier, inc=1, device_id={"box": other})

    permutation = interleave()

    place = col * own + lax.broadcasted_iota(jnp.int32, (own, 8, LANES), 0)
    fine_alive = alive(place, groups, live_fine)
    coarse_alive = alive(jnp.full((16, LANES), col, jnp.int32), coarse_groups, live_coarse)

    def cut(j, carry):
        lanes = pl.ds(pl.multiple_of(j * LANES, LANES), LANES)
        parts = [
            jnp.where(fine_alive, fine_ref[:, c, :, lanes].astype(jnp.float32), 0.0) for c in range(2)
        ]
        outbox[j] = by_band(parts, permutation).reshape(PAIRS, 2 * own, WIDE)
        both = jnp.concatenate(
            [coarse_ref[0, c, :, lanes].astype(jnp.float32) for c in range(2)], axis=0
        )
        outbox_coarse[j] = jnp.where(coarse_alive, both, 0.0).astype(jnp.bfloat16)
        return carry

    lax.fori_loop(0, n_freq, cut, 0)

    pl.semaphore_wait(barrier, n_freq + 1)

    def coarse_copy(step):
        peer = lax.rem(col + step, n_freq)
        return pltpu.make_async_remote_copy(
            src_ref=outbox_coarse.at[peer],
            dst_ref=held_coarse.at[RIM_COARSE + col],
            send_sem=coarse_send.at[step],
            recv_sem=coarse_recv.at[step],
            device_id={"freq": peer},
        )

    def fine_copy(pair, step):
        peer = lax.rem(col + step, n_freq)
        return pltpu.make_async_remote_copy(
            src_ref=outbox.at[peer, pair],
            dst_ref=held.at[pair, 2 + col],
            send_sem=send_sem.at[pair, step],
            recv_sem=recv_sem.at[pair, step],
            device_id={"freq": peer},
        )

    def coarse_rim_copy(up):
        first, landing = (coarse_groups, 0) if up else (RIM_COARSE, RIM_COARSE + coarse_groups)
        return pltpu.make_async_remote_copy(
            src_ref=held_coarse.at[pl.ds(first, RIM_COARSE)],
            dst_ref=held_coarse.at[pl.ds(landing, RIM_COARSE)],
            send_sem=coarse_rim_send.at[int(up)],
            recv_sem=coarse_rim_recv.at[int(up)],
            device_id={"box": above if up else below},
        )

    def rim_copy(pair, up):
        first, landing = (n_freq, 0) if up else (2, 2 + n_freq)
        return pltpu.make_async_remote_copy(
            src_ref=held.at[pair, pl.ds(first, 2)],
            dst_ref=held.at[pair, pl.ds(landing, 2)],
            send_sem=rim_send.at[pair, int(up)],
            recv_sem=rim_recv.at[pair, int(up)],
            device_id={"box": above if up else below},
        )

    for step in order:
        coarse_copy(step).start()
    for pair in range(PAIRS):
        for step in order:
            fine_copy(pair, step).start()
    held_coarse[RIM_COARSE + col] = outbox_coarse[col]
    for pair in range(PAIRS):
        held[pair, 2 + col] = outbox[col, pair]
        held[pair, 14] = jnp.zeros((16, WIDE), jnp.bfloat16)
        held[pair, 15] = jnp.zeros((16, WIDE), jnp.bfloat16)
    for blank in range(2 * RIM_COARSE + coarse_groups, 16):
        held_coarse[blank] = jnp.zeros((16, LANES), jnp.bfloat16)

    fine_list = lists_fine_ref[...]
    fine_at = fine_list - (box * groups - RIM_FINE)
    fine_row = jnp.where(fine_list >= 0, (fine_at // 8) * 16 + fine_at % 8, -1000)
    coarse_list = lists_coarse_ref[...]
    coarse_at = coarse_list - (box * coarse_groups - RIM_COARSE)
    coarse_row = jnp.where(coarse_list >= 0, 192 + coarse_at, -1000)
    lane_fine = lax.broadcasted_iota(jnp.int32, (groups, WIDE), 1)
    lane_coarse = lax.broadcasted_iota(jnp.int32, (coarse_groups, WIDE), 1)
    no_rows = jnp.zeros((16 - coarse_groups, WIDE), jnp.float32)
    for k in range(slots):
        for odd in range(2):
            picks[odd, pl.ds(k * rows, groups)] = jnp.where(
                fine_row[:, k : k + 1] + 8 * odd == lane_fine, 1.0, 0.0
            ).astype(jnp.bfloat16)
            coarse_hit = jnp.where(coarse_row[:, k : k + 1] + 16 * odd == lane_coarse, 1.0, 0.0)
            picks[odd, pl.ds(k * rows + groups, 16)] = jnp.concatenate(
                [coarse_hit, no_rows], axis=0
            ).astype(jnp.bfloat16)

    lane_band = lax.broadcasted_iota(jnp.int32, (16, WIDE), 1) % BAND

    def widen(k, carry):
        table = [
            swap_blocks([table_ref[k, c, o].astype(jnp.float32) for o in range(8)]) for c in range(2)
        ]
        for g in range(BANDS):
            real, imag = table[0][g], table[1][g]
            full = jnp.concatenate(
                [
                    jnp.concatenate([real, imag], axis=1),
                    jnp.concatenate([-imag, real], axis=1),
                ],
                axis=0,
            ).astype(jnp.bfloat16)
            for f in range(BAND):
                weights[g, k, pl.ds(f * 16, 16)] = jnp.where(lane_band == f, full, jnp.zeros_like(full))
        return carry

    lax.fori_loop(0, slots, widen, 0)

    for step in order:
        coarse_copy(step).wait_recv()
    for up in (True, False):
        coarse_rim_copy(up).start()
    for up in (True, False):
        coarse_rim_copy(up).wait_recv()
    coarse_parts = [held_coarse[:, pl.ds(8 * c, 8)].astype(jnp.float32) for c in range(2)]
    coarse_bands = by_band(coarse_parts, permutation)
    for g in range(BANDS):
        held[g // 2, 12 + g % 2] = coarse_bands[16 * g : 16 * g + 16]

    def advance(turn, carry):
        @pl.when(turn < PAIRS)
        def _():
            for step in order:
                fine_copy(turn, step).wait_recv()
            for up in (True, False):
                rim_copy(turn, up).start()

        @pl.when(turn > 0)
        def _():
            pair = turn - 1
            for up in (True, False):
                rim_copy(pair, up).wait_recv()
            sources = held[pair].reshape(16 * 16, WIDE)
            for odd in range(2):
                gathered[...] = jnp.dot(
                    picks[odd], sources, preferred_element_type=jnp.float32
                ).astype(jnp.bfloat16)
                total = jnp.zeros((rows, WIDE), jnp.float32)
                for k in range(slots):
                    total = total + jnp.dot(
                        gathered[pl.ds(k * rows, rows)],
                        weights[2 * pair + odd, k],
                        preferred_element_type=jnp.float32,
                    )
                sums[2 * pair + odd] = total

        return carry

    lax.fori_loop(0, PAIRS + 1, advance, 0)

    def back(first, live, count, scale):
        keep = alive(first + lax.broadcasted_iota(jnp.int32, (8, 8, LANES), 0), count, live)
        result = []
        for c in range(2):
            planes = swap_blocks(
                [sums[g, pl.ds(first + scale[1], 8), pl.ds(c * LANES, LANES)] for g in range(BANDS)]
            )
            turned = jnp.swapaxes(jnp.stack(planes, axis=0), 0, 1)
            result.append(jnp.where(keep, scale[0] * turned, 0.0).astype(jnp.bfloat16))
        return result

    def finish(part, carry):
        first = pl.multiple_of(part * 8, 8)
        result = back(first, live_fine, groups, (1.0, 0))
        for c in range(2):
            out_fine_ref[pl.ds(first, 8), c] = result[c]
        return carry

    lax.fori_loop(0, groups // 8, finish, 0)
    result = back(0, live_coarse, coarse_groups, (0.5, groups))
    for c in range(2):
        out_coarse_ref[:, c] = result[c]

    for step in order:
        coarse_copy(step).wait_send()
        for pair in range(PAIRS):
            fine_copy(pair, step).wait_send()
    for up in (True, False):
        coarse_rim_copy(up).wait_send()
        for pair in range(PAIRS):
            rim_copy(pair, up).wait_send()


def per_device(n_box, n_freq, spectra_fine, spectra_coarse, kernel_table, lists_fine, lists_coarse, live_counts):
    groups, slots = lists_fine.shape
    coarse_groups = lists_coarse.shape[0]
    own = spectra_fine.shape[0]
    rows = groups + 16
    vmem = pl.BlockSpec(memory_space=pltpu.VMEM)
    dma = pltpu.SemaphoreType.DMA
    return pl.pallas_call(
        functools.partial(kernel, n_box, n_freq),
        out_shape=(
            jax.ShapeDtypeStruct((groups, 2, 8, LANES), jnp.bfloat16),
            jax.ShapeDtypeStruct((coarse_groups, 2, 8, LANES), jnp.bfloat16),
        ),
        in_specs=[pl.BlockSpec(memory_space=pltpu.SMEM)] + [vmem] * 5,
        out_specs=(vmem, vmem),
        scratch_shapes=[
            pltpu.VMEM((n_freq, PAIRS, 2 * own, WIDE), jnp.bfloat16),
            pltpu.VMEM((n_freq, 16, LANES), jnp.bfloat16),
            pltpu.VMEM((PAIRS, 16, 16, WIDE), jnp.bfloat16),
            pltpu.VMEM((16, 16, LANES), jnp.bfloat16),
            pltpu.VMEM((2, slots * rows, WIDE), jnp.bfloat16),
            pltpu.VMEM((BANDS, slots, WIDE, WIDE), jnp.bfloat16),
            pltpu.VMEM((slots * rows, WIDE), jnp.bfloat16),
            pltpu.VMEM((BANDS, rows, WIDE), jnp.float32),
            dma((PAIRS, n_freq)),
            dma((PAIRS, n_freq)),
            dma((PAIRS, 2)),
            dma((PAIRS, 2)),
            dma((n_freq,)),
            dma((n_freq,)),
            dma((2,)),
            dma((2,)),
        ],
        compiler_params=pltpu.CompilerParams(
            collective_id=0, has_side_effects=True, vmem_limit_bytes=56 * 1024 * 1024
        ),
    )(live_counts, spectra_fine, spectra_coarse, kernel_table, lists_fine, lists_coarse)


def solution(mesh):
    return jax.shard_map(
        functools.partial(per_device, mesh.shape["box"], mesh.shape["freq"]),
        mesh=mesh,
        in_specs=(
            P(("box", "freq"), None, None, None),
            P(("box", "freq"), None, None, None),
            P(None, None, None, None, "freq"),
            P("box", None),
            P("box", None),
            P("box", None),
        ),
        out_specs=(P("box", None, None, "freq"), P("box", None, None, "freq")),
        check_vma=False,
    )
```

time: 245 us -> 66.5 us (0.27)
  the two profiles are of different devices: /device:TPU:475 before, /device:TPU:64 now
where the time goes in v1:
time: 66.5 us; the launch traced here: 66.3 us
  Pallas kernels  62 us (93%)
  local copies, waits for them, and re-layouts  3.71 us (6%)
    pallas_call x1, Pallas kernels, per_device(): pl.pallas_call(functools.partial(kernel, n_box, n_freq), out_shape=(jax.S...  62 us
    unnamed x5, local copies, waits for them, and re-layouts  3.71 us

profile of v1, /device:TPU:64, one launch (start us, length us, event | category | flops | bytes accessed | tf_op | source)
XLA Modules:
  0.0 66.3 jit_solution(4808562306954048375)
XLA Ops:
  0.6 1.4 %copy.8.lists_fine_ref = s32[64,26]{1,0:T(8,128)} copy(s32[64,26]{0,1:T(8,128)} %param.9) | data formatting | bytes 13312 | tf_op args[3]
  2.0 62.0 %shard_map.77 = (bf16[64,2,8,128]{3,2,1,0:T(8,128)(2,1)}, bf16[8,2,8,128]{3,2,1,0:T(8,128)(2,1)}) custom-call(s32[1,2]{1,0:T(1,128)} %live_ref.1, bf16[8,2,8,1024]{3,2,1,0:T(8,128)(2,1)} %fine_ref.1, bf16[1,2,8,1024]{3,2,1,0:T(8,128)(2,1)} %coarse_ref.1, bf16[26,2,8,8,128]{4,3,2,1,0:T(8,128)(2,1)} %table_ref.1, s32[64,26]{1,0:T(8,128)} %copy.8.lists_fine_ref, ...), custom_call_target="tpu_custom_call" | custom-call | tf_op jit(solution)/shard_map/pallas_call | solution.py:299
  64.0 0.0 copy-start
  64.0 1.7 %copy.11 = bf16[64,2,8,128]{3,2,1,0:T(8,128)(2,1)} copy(bf16[64,2,8,128]{3,2,1,0:T(8,128)(2,1)} %get-tuple-element.4) | data formatting | bytes 524288
  65.7 0.0 copy-done
  65.7 0.6 copy.12
Async XLA Ops:
  64.0 1.7 %copy-start = (bf16[8,2,8,128]{3,2,1,0:T(8,128)(2,1)S(1)}, bf16[8,2,8,128]{3,2,1,0:T(8,128)(2,1)}, u32[]{:S(2)}) copy-start(bf16[8,2,8,128]{3,2,1,0:T(8,128)(2,1)} %get-tuple-element.5) | copy-start | bytes 98308

commit v2 on v1

--- a/solution.py
+++ b/solution.py
@@ -9,6 +9,7 @@
 
 RIM_FINE = 16
 RIM_COARSE = 2
+HALF = 8
 LANES = 128
 BAND = 16
 BANDS = LANES // BAND
@@ -79,25 +80,54 @@
     coarse_recv,
     coarse_rim_send,
     coarse_rim_recv,
+    far_send,
+    far_recv,
 ):
     box = lax.axis_index("box")
     col = lax.axis_index("freq")
     above = lax.rem(box + 1, n_box)
     below = lax.rem(box + n_box - 1, n_box)
     slots = table_ref.shape[0]
-    groups = lists_fine_ref.shape[0]
-    coarse_groups = lists_coarse_ref.shape[0]
+    groups = lists_fine_ref.shape[1]
+    coarse_groups = lists_coarse_ref.shape[1]
     own = fine_ref.shape[0]
     rows = groups + 16
     live_fine = live_ref[0, 0]
     live_coarse = live_ref[0, 1]
     order = (4, 3, 5, 2, 6, 1, 7)
 
+    has_above, has_below = box < n_box - 1, box > 0
+    far_above = has_above & (lax.rem(box, HALF) == HALF - 1)
+    far_below = has_below & (lax.rem(box, HALF) == 0)
+    near_above = has_above & (lax.rem(box, HALF) != HALF - 1)
+    near_below = has_below & (lax.rem(box, HALF) != 0)
+    gives_above = far_above & (col >= n_freq - 2)
+    gives_below = far_below & (col < 2)
+
     barrier = pltpu.get_barrier_semaphore()
     for step in range(1, n_freq):
         pl.semaphore_signal(barrier, inc=1, device_id={"freq": lax.rem(col + step, n_freq)})
-    for other in (above, below):
-        pl.semaphore_signal(barrier, inc=1, device_id={"box": other})
+    for near, other in ((near_above, above), (near_below, below)):
+
+        @pl.when(near)
+        def _():
+            pl.semaphore_signal(barrier, inc=1, device_id={"box": other})
+
+    for far, other, first in ((far_above, above, 0), (far_below, below, n_freq - 2)):
+
+        @pl.when(far)
+        def _():
+            for i in range(2):
+                pl.semaphore_signal(barrier, inc=1, device_id={"box": other, "freq": first + i})
+
+    ready = (
+        n_freq
+        - 1
+        + near_above.astype(jnp.int32)
+        + near_below.astype(jnp.int32)
+        + n_freq * gives_above.astype(jnp.int32)
+        + n_freq * gives_below.astype(jnp.int32)
+    )
 
     permutation = interleave()
 
@@ -117,9 +147,9 @@
         outbox_coarse[j] = jnp.where(coarse_alive, both, 0.0).astype(jnp.bfloat16)
         return carry
 
-    lax.fori_loop(0, n_freq, cut, 0)
-
-    pl.semaphore_wait(barrier, n_freq + 1)
+    lax.fori_loop(0, n_freq, cut, 0, unroll=True)
+
+    pl.semaphore_wait(barrier, ready)
 
     def coarse_copy(step):
         peer = lax.rem(col + step, n_freq)
@@ -161,9 +191,52 @@
             device_id={"box": above if up else below},
         )
 
+    def far_copies(up, pair):
+        if up:
+            other, landing, index = above, col - (n_freq - 2), lax.rem(col, 2)
+        else:
+            other, landing, index = below, n_freq + 2 + col, lax.rem(col, 2)
+        copies = []
+        for j in range(n_freq):
+            if pair is None:
+                source, target = outbox_coarse.at[j], held_coarse.at[landing]
+            else:
+                source, target = outbox.at[j, pair], held.at[pair, landing]
+            lot = PAIRS if pair is None else pair
+            copies.append(
+                pltpu.make_async_remote_copy(
+                    src_ref=source,
+                    dst_ref=target,
+                    send_sem=far_send.at[int(up), lot, j],
+                    recv_sem=far_recv.at[int(up), lot, index],
+                    device_id={"box": other, "freq": j},
+                )
+            )
+        return copies
+
+    def far_wait(up, pair):
+        for i in range(2):
+            landing = i if up else n_freq + 2 + i
+            if pair is None:
+                here = held_coarse.at[landing]
+            else:
+                here = held.at[pair, landing]
+            lot = PAIRS if pair is None else pair
+            pltpu.make_async_copy(here, here, far_recv.at[int(up), lot, i]).wait()
+
+    def start_far(pair):
+        for up, gives in ((True, gives_above), (False, gives_below)):
+
+            @pl.when(gives)
+            def _():
+                for copy in far_copies(up, pair):
+                    copy.start()
+
+    start_far(None)
     for step in order:
         coarse_copy(step).start()
     for pair in range(PAIRS):
+        start_far(pair)
         for step in order:
             fine_copy(pair, step).start()
     held_coarse[RIM_COARSE + col] = outbox_coarse[col]
@@ -171,13 +244,30 @@
         held[pair, 2 + col] = outbox[col, pair]
         held[pair, 14] = jnp.zeros((16, WIDE), jnp.bfloat16)
         held[pair, 15] = jnp.zeros((16, WIDE), jnp.bfloat16)
+
+    @pl.when(jnp.logical_not(has_below))
+    def _():
+        for pair in range(PAIRS):
+            for i in range(2):
+                held[pair, i] = jnp.zeros((16, WIDE), jnp.bfloat16)
+        for i in range(2):
+            held_coarse[i] = jnp.zeros((16, LANES), jnp.bfloat16)
+
+    @pl.when(jnp.logical_not(has_above))
+    def _():
+        for pair in range(PAIRS):
+            for i in range(2):
+                held[pair, n_freq + 2 + i] = jnp.zeros((16, WIDE), jnp.bfloat16)
+        for i in range(2):
+            held_coarse[n_freq + 2 + i] = jnp.zeros((16, LANES), jnp.bfloat16)
+
     for blank in range(2 * RIM_COARSE + coarse_groups, 16):
         held_coarse[blank] = jnp.zeros((16, LANES), jnp.bfloat16)
 
-    fine_list = lists_fine_ref[...]
+    fine_list = jnp.transpose(lists_fine_ref[...])
     fine_at = fine_list - (box * groups - RIM_FINE)
     fine_row = jnp.where(fine_list >= 0, (fine_at // 8) * 16 + fine_at % 8, -1000)
-    coarse_list = lists_coarse_ref[...]
+    coarse_list = jnp.transpose(lists_coarse_ref[...])
     coarse_at = coarse_list - (box * coarse_groups - RIM_COARSE)
     coarse_row = jnp.where(coarse_list >= 0, 192 + coarse_at, -1000)
     lane_fine = lax.broadcasted_iota(jnp.int32, (groups, WIDE), 1)
@@ -212,49 +302,63 @@
                 weights[g, k, pl.ds(f * 16, 16)] = jnp.where(lane_band == f, full, jnp.zeros_like(full))
         return carry
 
-    lax.fori_loop(0, slots, widen, 0)
+    lax.fori_loop(0, slots, widen, 0, unroll=2)
+
+    def rim_start(copy):
+        for up, near in ((True, near_above), (False, near_below)):
+
+            @pl.when(near)
+            def _():
+                copy(up).start()
+
+    def rim_wait(copy, pair):
+        for up, near, far in ((True, near_below, far_below), (False, near_above, far_above)):
+
+            @pl.when(near)
+            def _():
+                copy(up).wait_recv()
+
+            @pl.when(far)
+            def _():
+                far_wait(up, pair)
+
+    def arrive(pair):
+        for step in order:
+            fine_copy(pair, step).wait_recv()
+        rim_start(lambda up: rim_copy(pair, up))
 
     for step in order:
         coarse_copy(step).wait_recv()
-    for up in (True, False):
-        coarse_rim_copy(up).start()
-    for up in (True, False):
-        coarse_rim_copy(up).wait_recv()
+    rim_start(coarse_rim_copy)
+    arrive(0)
+    rim_wait(coarse_rim_copy, None)
     coarse_parts = [held_coarse[:, pl.ds(8 * c, 8)].astype(jnp.float32) for c in range(2)]
     coarse_bands = by_band(coarse_parts, permutation)
     for g in range(BANDS):
         held[g // 2, 12 + g % 2] = coarse_bands[16 * g : 16 * g + 16]
 
-    def advance(turn, carry):
-        @pl.when(turn < PAIRS)
+    def advance(pair, carry):
+        @pl.when(pair < PAIRS - 1)
         def _():
-            for step in order:
-                fine_copy(turn, step).wait_recv()
-            for up in (True, False):
-                rim_copy(turn, up).start()
-
-        @pl.when(turn > 0)
-        def _():
-            pair = turn - 1
-            for up in (True, False):
-                rim_copy(pair, up).wait_recv()
-            sources = held[pair].reshape(16 * 16, WIDE)
-            for odd in range(2):
-                gathered[...] = jnp.dot(
-                    picks[odd], sources, preferred_element_type=jnp.float32
-                ).astype(jnp.bfloat16)
-                total = jnp.zeros((rows, WIDE), jnp.float32)
-                for k in range(slots):
-                    total = total + jnp.dot(
-                        gathered[pl.ds(k * rows, rows)],
-                        weights[2 * pair + odd, k],
-                        preferred_element_type=jnp.float32,
-                    )
-                sums[2 * pair + odd] = total
-
+            arrive(pair + 1)
+
+        rim_wait(lambda up: rim_copy(pair, up), pair)
+        sources = held[pair].reshape(16 * 16, WIDE)
+        for odd in range(2):
+            gathered[...] = jnp.dot(
+                picks[odd], sources, preferred_element_type=jnp.float32
+            ).astype(jnp.bfloat16)
+            total = jnp.zeros((rows, WIDE), jnp.float32)
+            for k in range(slots):
+                total = total + jnp.dot(
+                    gathered[pl.ds(k * rows, rows)],
+                    weights[2 * pair + odd, k],
+                    preferred_element_type=jnp.float32,
+                )
+            sums[2 * pair + odd] = total
         return carry
 
-    lax.fori_loop(0, PAIRS + 1, advance, 0)
+    lax.fori_loop(0, PAIRS, advance, 0)
 
     def back(first, live, count, scale):
         keep = alive(first + lax.broadcasted_iota(jnp.int32, (8, 8, LANES), 0), count, live)
@@ -274,7 +378,7 @@
             out_fine_ref[pl.ds(first, 8), c] = result[c]
         return carry
 
-    lax.fori_loop(0, groups // 8, finish, 0)
+    lax.fori_loop(0, groups // 8, finish, 0, unroll=True)
     result = back(0, live_coarse, coarse_groups, (0.5, groups))
     for c in range(2):
         out_coarse_ref[:, c] = result[c]
@@ -283,10 +387,19 @@
         coarse_copy(step).wait_send()
         for pair in range(PAIRS):
             fine_copy(pair, step).wait_send()
-    for up in (True, False):
-        coarse_rim_copy(up).wait_send()
-        for pair in range(PAIRS):
-            rim_copy(pair, up).wait_send()
+    for up, near, gives in ((True, near_above, gives_above), (False, near_below, gives_below)):
+
+        @pl.when(near)
+        def _():
+            coarse_rim_copy(up).wait_send()
+            for pair in range(PAIRS):
+                rim_copy(pair, up).wait_send()
+
+        @pl.when(gives)
+        def _():
+            for pair in (None, *range(PAIRS)):
+                for copy in far_copies(up, pair):
+                    copy.wait_send()
 
 
 def per_device(n_box, n_freq, spectra_fine, spectra_coarse, kernel_table, lists_fine, lists_coarse, live_counts):
@@ -321,11 +434,13 @@
             dma((n_freq,)),
             dma((2,)),
             dma((2,)),
+            dma((2, PAIRS + 1, n_freq)),
+            dma((2, PAIRS + 1, 2)),
         ],
         compiler_params=pltpu.CompilerParams(
             collective_id=0, has_side_effects=True, vmem_limit_bytes=56 * 1024 * 1024
         ),
-    )(live_counts, spectra_fine, spectra_coarse, kernel_table, lists_fine, lists_coarse)
+    )(live_counts, spectra_fine, spectra_coarse, kernel_table, lists_fine.T, lists_coarse.T)
 
 
 def solution(mesh):

time: 66.5 us -> 44.7 us (0.67)
  the two profiles are of different devices: /device:TPU:64 before, /device:TPU:1 now
where the time goes in v2:
time: 44.7 us; the launch traced here: 44.5 us
  Pallas kernels  40.2 us (90%)
  local copies, waits for them, and re-layouts  3.67 us (8%)
  between operations  0.65 us (1%)
    pallas_call x1, Pallas kernels, per_device(): pl.pallas_call(functools.partial(kernel, n_box, n_freq), out_shape=(jax.S...  40.2 us
    unnamed x5, local copies, waits for them, and re-layouts  3.67 us

profile of v2, /device:TPU:1, one launch (start us, length us, event | category | flops | bytes accessed | tf_op | source)
XLA Modules:
  0.0 44.5 jit_solution(1660408055371266796)
XLA Ops:
  0.6 1.4 %copy.8 = s32[8,26]{0,1:T(8,128)} copy(s32[8,26]{1,0:T(8,128)} %param.10) | data formatting | bytes 1664 | tf_op args[4]
  2.0 40.2 %shard_map.77 = (bf16[64,2,8,128]{3,2,1,0:T(8,128)(2,1)}, bf16[8,2,8,128]{3,2,1,0:T(8,128)(2,1)}) custom-call(s32[1,2]{1,0:T(1,128)} %live_ref.1, bf16[8,2,8,1024]{3,2,1,0:T(8,128)(2,1)} %fine_ref.1, bf16[1,2,8,1024]{3,2,1,0:T(8,128)(2,1)} %coarse_ref.1, bf16[26,2,8,8,128]{4,3,2,1,0:T(8,128)(2,1)} %table_ref.1, s32[26,64]{1,0:T(8,128)} %bitcast.3, ...), custom_call_target="tpu_custom_call" | custom-call | tf_op jit(solution)/shard_map/pallas_call | solution.py:412
  42.2 0.0 copy-start
  42.2 1.7 %copy.11 = bf16[64,2,8,128]{3,2,1,0:T(8,128)(2,1)} copy(bf16[64,2,8,128]{3,2,1,0:T(8,128)(2,1)} %get-tuple-element.4) | data formatting | bytes 524288
  43.9 0.0 copy-done
  43.9 0.6 %copy.12 = bf16[8,2,8,128]{3,2,1,0:T(8,128)(2,1)} copy(bf16[8,2,8,128]{3,2,1,0:T(8,128)(2,1)S(1)} %copy-done) | data formatting | bytes 65536
Async XLA Ops:
  42.2 1.7 %copy-start = (bf16[8,2,8,128]{3,2,1,0:T(8,128)(2,1)S(1)}, bf16[8,2,8,128]{3,2,1,0:T(8,128)(2,1)}, u32[]{:S(2)}) copy-start(bf16[8,2,8,128]{3,2,1,0:T(8,128)(2,1)} %get-tuple-element.5) | copy-start | bytes 98308

commit v3 on v2

--- a/solution.py
+++ b/solution.py
@@ -82,6 +82,8 @@
     coarse_rim_recv,
     far_send,
     far_recv,
+    ready_sem,
+    far_ready,
 ):
     box = lax.axis_index("box")
     col = lax.axis_index("freq")
@@ -94,7 +96,7 @@
     rows = groups + 16
     live_fine = live_ref[0, 0]
     live_coarse = live_ref[0, 1]
-    order = (4, 3, 5, 2, 6, 1, 7)
+    steps = tuple(range(1, n_freq))
 
     has_above, has_below = box < n_box - 1, box > 0
     far_above = has_above & (lax.rem(box, HALF) == HALF - 1)
@@ -104,29 +106,28 @@
     gives_above = far_above & (col >= n_freq - 2)
     gives_below = far_below & (col < 2)
 
+    first, last = col == 0, col == n_freq - 1
+    early = lax.rem(box // HALF, 2) == 0
+
+    def signal(semaphore, **device):
+        pl.semaphore_signal(semaphore, inc=1, device_id=device)
+
     barrier = pltpu.get_barrier_semaphore()
-    for step in range(1, n_freq):
-        pl.semaphore_signal(barrier, inc=1, device_id={"freq": lax.rem(col + step, n_freq)})
     for near, other in ((near_above, above), (near_below, below)):
 
         @pl.when(near)
         def _():
-            pl.semaphore_signal(barrier, inc=1, device_id={"box": other})
-
-    for far, other, first in ((far_above, above, 0), (far_below, below, n_freq - 2)):
-
-        @pl.when(far)
-        def _():
-            for i in range(2):
-                pl.semaphore_signal(barrier, inc=1, device_id={"box": other, "freq": first + i})
+            signal(barrier, box=other)
+
+    @pl.when(gives_below)
+    def _():
+        signal(barrier, box=below, freq=n_freq - 1)
 
     ready = (
-        n_freq
-        - 1
+        jnp.where(first, 0, 1)
         + near_above.astype(jnp.int32)
         + near_below.astype(jnp.int32)
-        + n_freq * gives_above.astype(jnp.int32)
-        + n_freq * gives_below.astype(jnp.int32)
+        + jnp.where(far_above & last, 2, 0)
     )
 
     permutation = interleave()
@@ -150,6 +151,21 @@
     lax.fori_loop(0, n_freq, cut, 0, unroll=True)
 
     pl.semaphore_wait(barrier, ready)
+
+    @pl.when(jnp.logical_not(last))
+    def _():
+        signal(barrier, freq=col + 1)
+
+    for step in steps:
+
+        @pl.when(col >= step)
+        def _():
+            signal(ready_sem.at[step], freq=col - step)
+
+    @pl.when(far_above & last)
+    def _():
+        for i in range(2):
+            signal(far_ready.at[0], box=above, freq=i)
 
     def coarse_copy(step):
         peer = lax.rem(col + step, n_freq)
@@ -224,21 +240,48 @@
             lot = PAIRS if pair is None else pair
             pltpu.make_async_copy(here, here, far_recv.at[int(up), lot, i]).wait()
 
-    def start_far(pair):
+    for pair in (None, *range(PAIRS)):
+        for step in steps:
+
+            @pl.when(col + step >= n_freq)
+            def _():
+                (coarse_copy(step) if pair is None else fine_copy(pair, step)).start()
+
+    def send_on():
+        for step in steps:
+
+            @pl.when(col + step < n_freq)
+            def _():
+                pl.semaphore_wait(ready_sem.at[step], 1)
+                coarse_copy(step).start()
+                for pair in range(PAIRS):
+                    fine_copy(pair, step).start()
+
+        @pl.when(gives_below)
+        def _():
+            pl.semaphore_wait(far_ready.at[0], 1)
+
+        @pl.when(far_below & first)
+        def _():
+            signal(far_ready.at[1], box=below, freq=n_freq - 1)
+
+        @pl.when(far_above & last)
+        def _():
+            pl.semaphore_wait(far_ready.at[1], 1)
+            signal(far_ready.at[2], freq=n_freq - 2)
+
+        @pl.when(far_above & (col == n_freq - 2))
+        def _():
+            pl.semaphore_wait(far_ready.at[2], 1)
+
         for up, gives in ((True, gives_above), (False, gives_below)):
 
             @pl.when(gives)
             def _():
-                for copy in far_copies(up, pair):
-                    copy.start()
-
-    start_far(None)
-    for step in order:
-        coarse_copy(step).start()
-    for pair in range(PAIRS):
-        start_far(pair)
-        for step in order:
-            fine_copy(pair, step).start()
+                for pair in (None, *range(PAIRS)):
+                    for copy in far_copies(up, pair):
+                        copy.start()
+
     held_coarse[RIM_COARSE + col] = outbox_coarse[col]
     for pair in range(PAIRS):
         held[pair, 2 + col] = outbox[col, pair]
@@ -264,45 +307,61 @@
     for blank in range(2 * RIM_COARSE + coarse_groups, 16):
         held_coarse[blank] = jnp.zeros((16, LANES), jnp.bfloat16)
 
-    fine_list = jnp.transpose(lists_fine_ref[...])
-    fine_at = fine_list - (box * groups - RIM_FINE)
-    fine_row = jnp.where(fine_list >= 0, (fine_at // 8) * 16 + fine_at % 8, -1000)
-    coarse_list = jnp.transpose(lists_coarse_ref[...])
-    coarse_at = coarse_list - (box * coarse_groups - RIM_COARSE)
-    coarse_row = jnp.where(coarse_list >= 0, 192 + coarse_at, -1000)
-    lane_fine = lax.broadcasted_iota(jnp.int32, (groups, WIDE), 1)
-    lane_coarse = lax.broadcasted_iota(jnp.int32, (coarse_groups, WIDE), 1)
-    no_rows = jnp.zeros((16 - coarse_groups, WIDE), jnp.float32)
-    for k in range(slots):
-        for odd in range(2):
-            picks[odd, pl.ds(k * rows, groups)] = jnp.where(
-                fine_row[:, k : k + 1] + 8 * odd == lane_fine, 1.0, 0.0
-            ).astype(jnp.bfloat16)
-            coarse_hit = jnp.where(coarse_row[:, k : k + 1] + 16 * odd == lane_coarse, 1.0, 0.0)
-            picks[odd, pl.ds(k * rows + groups, 16)] = jnp.concatenate(
-                [coarse_hit, no_rows], axis=0
-            ).astype(jnp.bfloat16)
-
-    lane_band = lax.broadcasted_iota(jnp.int32, (16, WIDE), 1) % BAND
-
-    def widen(k, carry):
-        table = [
-            swap_blocks([table_ref[k, c, o].astype(jnp.float32) for o in range(8)]) for c in range(2)
-        ]
-        for g in range(BANDS):
-            real, imag = table[0][g], table[1][g]
-            full = jnp.concatenate(
-                [
-                    jnp.concatenate([real, imag], axis=1),
-                    jnp.concatenate([-imag, real], axis=1),
-                ],
-                axis=0,
-            ).astype(jnp.bfloat16)
-            for f in range(BAND):
-                weights[g, k, pl.ds(f * 16, 16)] = jnp.where(lane_band == f, full, jnp.zeros_like(full))
+    def prepare():
+        fine_list = jnp.transpose(lists_fine_ref[...])
+        fine_at = fine_list - (box * groups - RIM_FINE)
+        fine_row = jnp.where(fine_list >= 0, (fine_at // 8) * 16 + fine_at % 8, -1000)
+        coarse_list = jnp.transpose(lists_coarse_ref[...])
+        coarse_at = coarse_list - (box * coarse_groups - RIM_COARSE)
+        coarse_row = jnp.where(coarse_list >= 0, 192 + coarse_at, -1000)
+        lane_fine = lax.broadcasted_iota(jnp.int32, (groups, WIDE), 1)
+        lane_coarse = lax.broadcasted_iota(jnp.int32, (coarse_groups, WIDE), 1)
+        no_rows = jnp.zeros((16 - coarse_groups, WIDE), jnp.float32)
+        for k in range(slots):
+            for odd in range(2):
+                picks[odd, pl.ds(k * rows, groups)] = jnp.where(
+                    fine_row[:, k : k + 1] + 8 * odd == lane_fine, 1.0, 0.0
+                ).astype(jnp.bfloat16)
+                coarse_hit = jnp.where(coarse_row[:, k : k + 1] + 16 * odd == lane_coarse, 1.0, 0.0)
+                picks[odd, pl.ds(k * rows + groups, 16)] = jnp.concatenate(
+                    [coarse_hit, no_rows], axis=0
+                ).astype(jnp.bfloat16)
+
+        lane_band = lax.broadcasted_iota(jnp.int32, (16, WIDE), 1) % BAND
+
+        def widen(k, carry):
+            table = [
+                swap_blocks([table_ref[k, c, o].astype(jnp.float32) for o in range(8)]) for c in range(2)
+            ]
+            for g in range(BANDS):
+                real, imag = table[0][g], table[1][g]
+                full = jnp.concatenate(
+                    [
+                        jnp.concatenate([real, imag], axis=1),
+                        jnp.concatenate([-imag, real], axis=1),
+                    ],
+                    axis=0,
+                ).astype(jnp.bfloat16)
+                for f in range(BAND):
+                    weights[g, k, pl.ds(f * 16, 16)] = jnp.where(lane_band == f, full, jnp.zeros_like(full))
+            return carry
+
+        lax.fori_loop(0, slots, widen, 0, unroll=2)
+
+    def middle(turn, carry):
+        local = (turn == 0) == early
+
+        @pl.when(local)
+        def _():
+            prepare()
+
+        @pl.when(jnp.logical_not(local))
+        def _():
+            send_on()
+
         return carry
 
-    lax.fori_loop(0, slots, widen, 0, unroll=2)
+    lax.fori_loop(0, 2, middle, 0)
 
     def rim_start(copy):
         for up, near in ((True, near_above), (False, near_below)):
@@ -323,11 +382,11 @@
                 far_wait(up, pair)
 
     def arrive(pair):
-        for step in order:
+        for step in steps:
             fine_copy(pair, step).wait_recv()
         rim_start(lambda up: rim_copy(pair, up))
 
-    for step in order:
+    for step in steps:
         coarse_copy(step).wait_recv()
     rim_start(coarse_rim_copy)
     arrive(0)
@@ -383,7 +442,7 @@
     for c in range(2):
         out_coarse_ref[:, c] = result[c]
 
-    for step in order:
+    for step in steps:
         coarse_copy(step).wait_send()
         for pair in range(PAIRS):
             fine_copy(pair, step).wait_send()
@@ -436,6 +495,8 @@
             dma((2,)),
             dma((2, PAIRS + 1, n_freq)),
             dma((2, PAIRS + 1, 2)),
+            pltpu.SemaphoreType.REGULAR((n_freq,)),
+            pltpu.SemaphoreType.REGULAR((3,)),
         ],
         compiler_params=pltpu.CompilerParams(
             collective_id=0, has_side_effects=True, vmem_limit_bytes=56 * 1024 * 1024

time: 44.7 us -> 48.7 us (1.089)
  the two profiles are of different devices: /device:TPU:1 before, /device:TPU:29 now
where the time goes in v3:
time: 48.7 us; the launch traced here: 48.5 us
  Pallas kernels  44.2 us (91%)
  local copies, waits for them, and re-layouts  3.67 us (8%)
  between operations  0.65 us (1%)
    pallas_call x1, Pallas kernels, per_device(): pl.pallas_call(functools.partial(kernel, n_box, n_freq), out_shape=(jax.S...  44.2 us
    unnamed x5, local copies, waits for them, and re-layouts  3.67 us

profile of v3, /device:TPU:29, one launch (start us, length us, event | category | flops | bytes accessed | tf_op | source)
XLA Modules:
  0.0 48.5 jit_solution(13890435551654938415)
XLA Ops:
  0.6 1.4 %copy.8 = s32[8,26]{0,1:T(8,128)} copy(s32[8,26]{1,0:T(8,128)} %param.10) | data formatting | bytes 1664 | tf_op args[4]
  2.0 44.2 %shard_map.77 = (bf16[64,2,8,128]{3,2,1,0:T(8,128)(2,1)}, bf16[8,2,8,128]{3,2,1,0:T(8,128)(2,1)}) custom-call(s32[1,2]{1,0:T(1,128)} %live_ref.1, bf16[8,2,8,1024]{3,2,1,0:T(8,128)(2,1)} %fine_ref.1, bf16[1,2,8,1024]{3,2,1,0:T(8,128)(2,1)} %coarse_ref.1, bf16[26,2,8,8,128]{4,3,2,1,0:T(8,128)(2,1)} %table_ref.1, s32[26,64]{1,0:T(8,128)} %bitcast.3, ...), custom_call_target="tpu_custom_call" | custom-call | tf_op jit(solution)/shard_map/pallas_call | solution.py:471
  46.2 0.0 copy-start
  46.2 1.7 %copy.11 = bf16[64,2,8,128]{3,2,1,0:T(8,128)(2,1)} copy(bf16[64,2,8,128]{3,2,1,0:T(8,128)(2,1)} %get-tuple-element.4) | data formatting | bytes 524288
  47.9 0.0 copy-done
  47.9 0.6 %copy.12 = bf16[8,2,8,128]{3,2,1,0:T(8,128)(2,1)} copy(bf16[8,2,8,128]{3,2,1,0:T(8,128)(2,1)S(1)} %copy-done) | data formatting | bytes 65536
Async XLA Ops:
  46.2 1.7 %copy-start = (bf16[8,2,8,128]{3,2,1,0:T(8,128)(2,1)S(1)}, bf16[8,2,8,128]{3,2,1,0:T(8,128)(2,1)}, u32[]{:S(2)}) copy-start(bf16[8,2,8,128]{3,2,1,0:T(8,128)(2,1)} %get-tuple-element.5) | copy-start | bytes 98308

commit v4 on v3

--- a/solution.py
+++ b/solution.py
@@ -106,7 +106,6 @@
     gives_above = far_above & (col >= n_freq - 2)
     gives_below = far_below & (col < 2)
 
-    first, last = col == 0, col == n_freq - 1
     early = lax.rem(box // HALF, 2) == 0
 
     def signal(semaphore, **device):
@@ -119,15 +118,39 @@
         def _():
             signal(barrier, box=other)
 
-    @pl.when(gives_below)
-    def _():
-        signal(barrier, box=below, freq=n_freq - 1)
-
+    for step in steps:
+
+        @pl.when(jnp.logical_not(early) | (col + step < n_freq))
+        def _():
+            signal(barrier, freq=lax.rem(col + step, n_freq))
+
+    for far, gives, other, giver in (
+        (far_above, gives_above, above, 0),
+        (far_below, gives_below, below, n_freq - 2),
+    ):
+
+        @pl.when(early & far)
+        def _():
+            for i in range(2):
+                signal(barrier, box=other, freq=giver + i)
+
+        @pl.when(early & gives)
+        def _():
+            for j in range(n_freq):
+                signal(barrier, box=other, freq=j)
+
+    late_ready = (
+        n_freq
+        - 1
+        + jnp.where(far_above, 2, 0)
+        + jnp.where(far_below, 2, 0)
+        + jnp.where(gives_above, n_freq, 0)
+        + jnp.where(gives_below, n_freq, 0)
+    )
     ready = (
-        jnp.where(first, 0, 1)
+        jnp.where(early, col, late_ready)
         + near_above.astype(jnp.int32)
         + near_below.astype(jnp.int32)
-        + jnp.where(far_above & last, 2, 0)
     )
 
     permutation = interleave()
@@ -152,20 +175,18 @@
 
     pl.semaphore_wait(barrier, ready)
 
-    @pl.when(jnp.logical_not(last))
-    def _():
-        signal(barrier, freq=col + 1)
-
     for step in steps:
 
-        @pl.when(col >= step)
+        @pl.when(early & (col >= step))
         def _():
             signal(ready_sem.at[step], freq=col - step)
 
-    @pl.when(far_above & last)
-    def _():
-        for i in range(2):
-            signal(far_ready.at[0], box=above, freq=i)
+    for far, other, giver in ((far_above, above, 0), (far_below, below, n_freq - 2)):
+
+        @pl.when(jnp.logical_not(early) & far)
+        def _():
+            for i in range(2):
+                signal(far_ready, box=other, freq=giver + i)
 
     def coarse_copy(step):
         peer = lax.rem(col + step, n_freq)
@@ -252,27 +273,17 @@
 
             @pl.when(col + step < n_freq)
             def _():
-                pl.semaphore_wait(ready_sem.at[step], 1)
+                @pl.when(early)
+                def _():
+                    pl.semaphore_wait(ready_sem.at[step], 1)
+
                 coarse_copy(step).start()
                 for pair in range(PAIRS):
                     fine_copy(pair, step).start()
 
-        @pl.when(gives_below)
-        def _():
-            pl.semaphore_wait(far_ready.at[0], 1)
-
-        @pl.when(far_below & first)
-        def _():
-            signal(far_ready.at[1], box=below, freq=n_freq - 1)
-
-        @pl.when(far_above & last)
-        def _():
-            pl.semaphore_wait(far_ready.at[1], 1)
-            signal(far_ready.at[2], freq=n_freq - 2)
-
-        @pl.when(far_above & (col == n_freq - 2))
-        def _():
-            pl.semaphore_wait(far_ready.at[2], 1)
+        @pl.when(early & (gives_above | gives_below))
+        def _():
+            pl.semaphore_wait(far_ready, n_freq)
 
         for up, gives in ((True, gives_above), (False, gives_below)):
 
@@ -496,7 +507,7 @@
             dma((2, PAIRS + 1, n_freq)),
             dma((2, PAIRS + 1, 2)),
             pltpu.SemaphoreType.REGULAR((n_freq,)),
-            pltpu.SemaphoreType.REGULAR((3,)),
+            pltpu.SemaphoreType.REGULAR,
         ],
         compiler_params=pltpu.CompilerParams(
             collective_id=0, has_side_effects=True, vmem_limit_bytes=56 * 1024 * 1024

time: 48.7 us -> 46.7 us (0.959)
  the two profiles are of different devices: /device:TPU:29 before, /device:TPU:27 now
where the time goes in v4:
time: 46.7 us; the launch traced here: 46.5 us
  Pallas kernels  42.1 us (90%)
  local copies, waits for them, and re-layouts  3.67 us (8%)
  between operations  0.65 us (1%)
    pallas_call x1, Pallas kernels, per_device(): pl.pallas_call(functools.partial(kernel, n_box, n_freq), out_shape=(jax.S...  42.1 us
    unnamed x5, local copies, waits for them, and re-layouts  3.67 us

profile of v4, /device:TPU:27, one launch (start us, length us, event | category | flops | bytes accessed | tf_op | source)
XLA Modules:
  0.0 46.5 jit_solution(4698403606437328719)
XLA Ops:
  0.6 1.4 %copy.8 = s32[8,26]{0,1:T(8,128)} copy(s32[8,26]{1,0:T(8,128)} %param.10) | data formatting | bytes 1664 | tf_op args[4]
  2.0 42.1 %shard_map.77 = (bf16[64,2,8,128]{3,2,1,0:T(8,128)(2,1)}, bf16[8,2,8,128]{3,2,1,0:T(8,128)(2,1)}) custom-call(s32[1,2]{1,0:T(1,128)} %live_ref.1, bf16[8,2,8,1024]{3,2,1,0:T(8,128)(2,1)} %fine_ref.1, bf16[1,2,8,1024]{3,2,1,0:T(8,128)(2,1)} %coarse_ref.1, bf16[26,2,8,8,128]{4,3,2,1,0:T(8,128)(2,1)} %table_ref.1, s32[26,64]{1,0:T(8,128)} %bitcast.3, ...), custom_call_target="tpu_custom_call" | custom-call | tf_op jit(solution)/shard_map/pallas_call | solution.py:482
  44.2 0.0 copy-start
  44.2 1.7 %copy.11 = bf16[64,2,8,128]{3,2,1,0:T(8,128)(2,1)} copy(bf16[64,2,8,128]{3,2,1,0:T(8,128)(2,1)} %get-tuple-element.4) | data formatting | bytes 524288
  45.8 0.0 copy-done
  45.8 0.6 %copy.12 = bf16[8,2,8,128]{3,2,1,0:T(8,128)(2,1)} copy(bf16[8,2,8,128]{3,2,1,0:T(8,128)(2,1)S(1)} %copy-done) | data formatting | bytes 65536
Async XLA Ops:
  44.2 1.7 %copy-start = (bf16[8,2,8,128]{3,2,1,0:T(8,128)(2,1)S(1)}, bf16[8,2,8,128]{3,2,1,0:T(8,128)(2,1)}, u32[]{:S(2)}) copy-start(bf16[8,2,8,128]{3,2,1,0:T(8,128)(2,1)} %get-tuple-element.5) | copy-start | bytes 98308

commit v5 on v4

v5 whole, which is shorter than its diff:
```python
import functools

import jax
import jax.numpy as jnp
from jax import lax
from jax.experimental import pallas as pl
from jax.experimental.pallas import tpu as pltpu
from jax.sharding import PartitionSpec as P

RIM_FINE = 16
RIM_COARSE = 2
HALF = 8
LANES = 128
BAND = 16
BANDS = LANES // BAND
PAIRS = BANDS // 2
WIDE = 2 * 8 * BAND
HALF_BAND = BAND // 2
FIRST = LANES
PACK = FIRST + PAIRS * WIDE
PARTS = ((0, FIRST + 2 * WIDE), (FIRST + 2 * WIDE, 2 * WIDE))


def swap_blocks(planes):
    count = len(planes)
    width = LANES // count
    block = lax.broadcasted_iota(jnp.int32, planes[0].shape, 1) // width
    planes = list(planes)
    step = count // 2
    while step:
        upper = (block & step) != 0
        for p in range(count):
            if p & step == 0:
                first, second = planes[p], planes[p + step]
                planes[p] = jnp.where(upper, pltpu.roll(second, width * step, 1), first)
                planes[p + step] = jnp.where(upper, second, pltpu.roll(first, LANES - width * step, 1))
        step //= 2
    return planes


def interleave():
    row = lax.broadcasted_iota(jnp.int32, (WIDE, WIDE), 0)
    lane = lax.broadcasted_iota(jnp.int32, (WIDE, WIDE), 1)
    hit = (row // BAND == lane % BAND) & (row % BAND == lane // BAND)
    return jnp.where(hit, 1.0, 0.0).astype(jnp.bfloat16)


def by_band(parts, permutation):
    planes = []
    for part in parts:
        turned = jnp.swapaxes(part, 0, 1)
        planes.append(swap_blocks([turned[i] for i in range(8)]))
    stacked = jnp.concatenate(
        [jnp.concatenate([planes[0][g], planes[1][g]], axis=1) for g in range(BANDS)], axis=0
    ).astype(jnp.bfloat16)
    return jnp.dot(stacked, permutation, preferred_element_type=jnp.float32).astype(jnp.bfloat16)


def alive(place, count, live):
    lower = live // 2
    return (place < lower) | (place >= count - (live - lower))


def kernel(
    n_box,
    n_freq,
    live_ref,
    fine_ref,
    coarse_ref,
    table_ref,
    lists_fine_ref,
    lists_coarse_ref,
    sums,
    outbox,
    held,
    picks,
    weights,
    gathered0,
    gathered1,
    send_sem,
    recv_sem,
    rim_send,
    rim_recv,
    far_send,
    far_recv,
    ready_sem,
    far_ready,
):
    box = lax.axis_index("box")
    col = lax.axis_index("freq")
    above = lax.rem(box + 1, n_box)
    below = lax.rem(box + n_box - 1, n_box)
    slots = table_ref.shape[0]
    groups = lists_fine_ref.shape[1]
    coarse_groups = lists_coarse_ref.shape[0]
    own = fine_ref.shape[0]
    rows = groups + 16
    live_fine = live_ref[0, 0]
    live_coarse = live_ref[0, 1]
    steps = tuple(range(1, n_freq))
    order = (4, 3, 5, 2, 6, 1, 7)

    has_above, has_below = box < n_box - 1, box > 0
    far_above = has_above & (lax.rem(box, HALF) == HALF - 1)
    far_below = has_below & (lax.rem(box, HALF) == 0)
    near_above = has_above & (lax.rem(box, HALF) != HALF - 1)
    near_below = has_below & (lax.rem(box, HALF) != 0)
    gives_above = far_above & (col >= n_freq - 2)
    gives_below = far_below & (col < 2)

    early = lax.rem(box // HALF, 2) == 0
    late = jnp.logical_not(early)

    def signal(semaphore, **device):
        pl.semaphore_signal(semaphore, inc=1, device_id=device)

    barrier = pltpu.get_barrier_semaphore()
    for near, other in ((near_above, above), (near_below, below)):

        @pl.when(near)
        def _():
            signal(barrier, box=other)

    for step in steps:

        @pl.when(late | (col + step < n_freq))
        def _():
            signal(barrier, freq=lax.rem(col + step, n_freq))

    for far, gives, other, giver in (
        (far_above, gives_above, above, 0),
        (far_below, gives_below, below, n_freq - 2),
    ):

        @pl.when(early & far)
        def _():
            for i in range(2):
                signal(barrier, box=other, freq=giver + i)

        @pl.when(early & gives)
        def _():
            for j in range(n_freq):
                signal(barrier, box=other, freq=j)

    late_ready = (
        n_freq
        - 1
        + jnp.where(far_above, 2, 0)
        + jnp.where(far_below, 2, 0)
        + jnp.where(gives_above, n_freq, 0)
        + jnp.where(gives_below, n_freq, 0)
    )
    ready = (
        jnp.where(early, col, late_ready)
        + near_above.astype(jnp.int32)
        + near_below.astype(jnp.int32)
    )

    permutation = interleave()

    place = col * own + lax.broadcasted_iota(jnp.int32, (own, 8, LANES), 0)
    fine_alive = alive(place, groups, live_fine)
    coarse_alive = alive(jnp.full((16, LANES), col, jnp.int32), coarse_groups, live_coarse)

    def cut(j, carry):
        lanes = pl.ds(pl.multiple_of(j * LANES, LANES), LANES)
        parts = [
            jnp.where(fine_alive, fine_ref[:, c, :, lanes].astype(jnp.float32), 0.0) for c in range(2)
        ]
        bands = by_band(parts, permutation)
        both = jnp.concatenate(
            [coarse_ref[0, c, :, lanes].astype(jnp.float32) for c in range(2)], axis=0
        )
        both = jnp.where(coarse_alive, both, 0.0).astype(jnp.bfloat16)
        rows_of = [bands[16 * pair : 16 * pair + 16] for pair in range(PAIRS)]
        outbox[j] = jnp.concatenate([both, *rows_of], axis=1)
        return carry

    lax.fori_loop(0, n_freq, cut, 0, unroll=True)

    pl.semaphore_wait(barrier, ready)

    for step in steps:

        @pl.when(early & (col >= step))
        def _():
            signal(ready_sem.at[step], freq=col - step)

    for far, other, giver in ((far_above, above, 0), (far_below, below, n_freq - 2)):

        @pl.when(late & far)
        def _():
            for i in range(2):
                signal(far_ready, box=other, freq=giver + i)

    def lanes_of(part):
        return pl.ds(PARTS[part][0], PARTS[part][1])

    def swap_copy(part, step):
        peer = lax.rem(col + step, n_freq)
        return pltpu.make_async_remote_copy(
            src_ref=outbox.at[peer, :, lanes_of(part)],
            dst_ref=held.at[2 + col, :, lanes_of(part)],
            send_sem=send_sem.at[part, step],
            recv_sem=recv_sem.at[part, step],
            device_id={"freq": peer},
        )

    def rim_copy(part, up):
        first, landing = (n_freq, 0) if up else (2, 2 + n_freq)
        return pltpu.make_async_remote_copy(
            src_ref=held.at[pl.ds(first, 2), :, lanes_of(part)],
            dst_ref=held.at[pl.ds(landing, 2), :, lanes_of(part)],
            send_sem=rim_send.at[part, int(up)],
            recv_sem=rim_recv.at[part, int(up)],
            device_id={"box": above if up else below},
        )

    def far_copies(up, part):
        if up:
            other, landing = above, col - (n_freq - 2)
        else:
            other, landing = below, n_freq + 2 + col
        return [
            pltpu.make_async_remote_copy(
                src_ref=outbox.at[j, :, lanes_of(part)],
                dst_ref=held.at[landing, :, lanes_of(part)],
                send_sem=far_send.at[int(up), part, j],
                recv_sem=far_recv.at[int(up), part, lax.rem(col, 2)],
                device_id={"box": other, "freq": j},
            )
            for j in range(n_freq)
        ]

    def far_wait(up, part):
        for i in range(2):
            here = held.at[i if up else n_freq + 2 + i, :, lanes_of(part)]
            pltpu.make_async_copy(here, here, far_recv.at[int(up), part, i]).wait()

    def far_start(when):
        for up, gives in ((True, gives_above), (False, gives_below)):

            @pl.when(when & gives)
            def _():
                for part in range(len(PARTS)):
                    for copy in far_copies(up, part):
                        copy.start()

    far_start(late)
    for part in range(len(PARTS)):
        for step in order:

            @pl.when(late | (col + step >= n_freq))
            def _():
                swap_copy(part, step).start()

    def send_on():
        for step in steps:

            @pl.when(early & (col + step < n_freq))
            def _():
                pl.semaphore_wait(ready_sem.at[step], 1)
                for part in range(len(PARTS)):
                    swap_copy(part, step).start()

        @pl.when(early & (gives_above | gives_below))
        def _():
            pl.semaphore_wait(far_ready, n_freq)

        far_start(early)

    held[2 + col] = outbox[col]
    blank = jnp.zeros((16, PACK), jnp.bfloat16)
    for i in range(n_freq + 4, 16):
        held[i] = blank

    @pl.when(jnp.logical_not(has_below))
    def _():
        for i in range(2):
            held[i] = blank

    @pl.when(jnp.logical_not(has_above))
    def _():
        for i in range(2):
            held[n_freq + 2 + i] = blank

    def prepare():
        fine_list = jnp.transpose(lists_fine_ref[...])
        fine_at = fine_list - (box * groups - RIM_FINE)
        fine_row = jnp.where(fine_list >= 0, (fine_at // 8) * 16 + fine_at % 8, -1000)
        coarse_list = lists_coarse_ref[...]
        coarse_at = coarse_list - (box * coarse_groups - RIM_COARSE)
        coarse_row = jnp.where(coarse_list >= 0, 192 + coarse_at, -1000)
        lane_fine = lax.broadcasted_iota(jnp.int32, (groups, WIDE), 1)
        lane_coarse = lax.broadcasted_iota(jnp.int32, (coarse_groups, WIDE), 1)
        no_rows = jnp.zeros((16 - coarse_groups, WIDE), jnp.float32)
        for k in range(slots):
            for odd in range(2):
                picks[odd, pl.ds(k * rows, groups)] = jnp.where(
                    fine_row[:, k : k + 1] + 8 * odd == lane_fine, 1.0, 0.0
                ).astype(jnp.bfloat16)
                coarse_hit = jnp.where(coarse_row[:, k : k + 1] + 16 * odd == lane_coarse, 1.0, 0.0)
                picks[odd, pl.ds(k * rows + groups, 16)] = jnp.concatenate(
                    [coarse_hit, no_rows], axis=0
                ).astype(jnp.bfloat16)

        lane = lax.broadcasted_iota(jnp.int32, (16, LANES), 1) % HALF_BAND
        left = lax.broadcasted_iota(jnp.int32, (8, LANES), 1) < LANES // 2

        def widen(pair, carry):
            for i in range(2):
                planes = [
                    table_ref[2 * pair + i, c, o].astype(jnp.float32)
                    for c in range(2)
                    for o in range(8)
                ]
                for b, real in enumerate(swap_blocks(planes)):
                    turned = pltpu.roll(real, LANES // 2, 1)
                    imag = jnp.where(left, -turned, turned)
                    full = jnp.concatenate([real, imag], axis=0).astype(jnp.bfloat16)
                    for f in range(HALF_BAND):
                        weights[b, pair, pl.ds(i * LANES + f * 16, 16)] = jnp.where(
                            lane == f, full, jnp.zeros_like(full)
                        )
            return carry

        lax.fori_loop(0, slots // 2, widen, 0)

    def middle(turn, carry):
        local = (turn == 0) == (early & (col < n_freq // 2))

        @pl.when(local)
        def _():
            prepare()

        @pl.when(jnp.logical_not(local))
        def _():
            send_on()

        return carry

    lax.fori_loop(0, 2, middle, 0)

    def rim_wait(part):
        for up, near, far in ((True, near_below, far_below), (False, near_above, far_above)):

            @pl.when(near)
            def _():
                rim_copy(part, up).wait_recv()

            @pl.when(far)
            def _():
                far_wait(up, part)

    def arrive(part):
        for senders, up, near in (
            ((0, 1), False, near_below),
            ((n_freq - 2, n_freq - 1), True, near_above),
            (range(2, n_freq - 2), None, None),
        ):
            for j in senders:
                step = lax.rem(col + n_freq - j, n_freq)

                @pl.when(step > 0)
                def _():
                    swap_copy(part, step).wait_recv()

            if near is not None:

                @pl.when(near)
                def _():
                    rim_copy(part, up).start()

    arrive(0)
    rim_wait(0)
    raw = held[:, :, pl.ds(0, LANES)].astype(jnp.float32)
    coarse_bands = by_band([raw[:, 0:8], raw[:, 8:16]], permutation)
    for g in range(BANDS):
        held[n_freq + 4 + g % 2, :, pl.ds(FIRST + g // 2 * WIDE, WIDE)] = coarse_bands[16 * g : 16 * g + 16]

    def advance(pair, carry):
        @pl.when(pair == 1)
        def _():
            arrive(1)

        @pl.when(pair == 2)
        def _():
            rim_wait(1)

        lanes = pl.ds(pl.multiple_of(FIRST + pair * WIDE, LANES), WIDE)
        sources = held[:, :, lanes].reshape(16 * 16, WIDE)
        for odd, gathered in enumerate((gathered0, gathered1)):
            for m in range(0, slots * rows, 416):
                gathered[pl.ds(m, 416)] = jnp.dot(
                    picks[odd, pl.ds(m, 416)], sources, preferred_element_type=jnp.float32
                ).astype(jnp.bfloat16)
        for odd, gathered in enumerate((gathered0, gathered1)):
            for half in range(2):
                band = 4 * pair + 2 * odd + half
                side = pl.ds(half * LANES, LANES)
                total = jnp.zeros((rows, LANES), jnp.float32)
                for k in range(0, slots, 2):
                    both = jnp.concatenate(
                        [gathered[pl.ds((k + i) * rows, rows), side] for i in range(2)], axis=1
                    )
                    total = total + jnp.dot(
                        both, weights[band, k // 2], preferred_element_type=jnp.float32
                    )
                sums[band] = total
        return carry

    lax.fori_loop(0, PAIRS, advance, 0)

    for part in range(len(PARTS)):
        for step in steps:
            swap_copy(part, step).wait_send()
        for up, near, gives in ((True, near_above, gives_above), (False, near_below, gives_below)):

            @pl.when(near)
            def _():
                rim_copy(part, up).wait_send()

            @pl.when(gives)
            def _():
                for copy in far_copies(up, part):
                    copy.wait_send()


def unfold(live_ref, sums_ref, out_fine_ref, out_coarse_ref):
    groups = out_fine_ref.shape[0]
    coarse_groups = out_coarse_ref.shape[0]

    def back(first, place, live, count, scale):
        keep = alive(place + lax.broadcasted_iota(jnp.int32, (8, 8, LANES), 0), count, live)
        planes = swap_blocks([sums_ref[b, pl.ds(first, 8)] for b in range(2 * BANDS)])
        result = []
        for c in range(2):
            turned = jnp.swapaxes(jnp.stack(planes[8 * c : 8 * c + 8], axis=0), 0, 1)
            result.append(jnp.where(keep, scale * turned, 0.0).astype(jnp.bfloat16))
        return result

    for first in range(0, groups, 8):
        result = back(first, first, live_ref[0, 0], groups, 1.0)
        for c in range(2):
            out_fine_ref[pl.ds(first, 8), c] = result[c]
    result = back(groups, 0, live_ref[0, 1], coarse_groups, 0.5)
    for c in range(2):
        out_coarse_ref[:, c] = result[c]


def per_device(n_box, n_freq, spectra_fine, spectra_coarse, kernel_table, lists_fine, lists_coarse, live_counts):
    groups, slots = lists_fine.shape
    coarse_groups = lists_coarse.shape[0]
    own = spectra_fine.shape[0]
    rows = groups + 16
    vmem = pl.BlockSpec(memory_space=pltpu.VMEM)
    dma = pltpu.SemaphoreType.DMA
    sums = pl.pallas_call(
        functools.partial(kernel, n_box, n_freq),
        out_shape=jax.ShapeDtypeStruct((2 * BANDS, rows, LANES), jnp.float32),
        in_specs=[pl.BlockSpec(memory_space=pltpu.SMEM)] + [vmem] * 5,
        out_specs=vmem,
        scratch_shapes=[
            pltpu.VMEM((n_freq, 2 * own, PACK), jnp.bfloat16),
            pltpu.VMEM((16, 16, PACK), jnp.bfloat16),
            pltpu.VMEM((2, slots * rows, WIDE), jnp.bfloat16),
            pltpu.VMEM((2 * BANDS, slots // 2, WIDE, LANES), jnp.bfloat16),
            pltpu.VMEM((slots * rows, WIDE), jnp.bfloat16),
            pltpu.VMEM((slots * rows, WIDE), jnp.bfloat16),
            dma((len(PARTS), n_freq)),
            dma((len(PARTS), n_freq)),
            dma((len(PARTS), 2)),
            dma((len(PARTS), 2)),
            dma((2, len(PARTS), n_freq)),
            dma((2, len(PARTS), 2)),
            pltpu.SemaphoreType.REGULAR((n_freq,)),
            pltpu.SemaphoreType.REGULAR,
        ],
        compiler_params=pltpu.CompilerParams(
            collective_id=0, has_side_effects=True, vmem_limit_bytes=56 * 1024 * 1024
        ),
    )(live_counts, spectra_fine, spectra_coarse, kernel_table, lists_fine.T, lists_coarse)
    return pl.pallas_call(
        unfold,
        out_shape=(
            jax.ShapeDtypeStruct((groups, 2, 8, LANES), jnp.bfloat16),
            jax.ShapeDtypeStruct((coarse_groups, 2, 8, LANES), jnp.bfloat16),
        ),
        in_specs=[pl.BlockSpec(memory_space=pltpu.SMEM), vmem],
        out_specs=(vmem, vmem),
        compiler_params=pltpu.CompilerParams(vmem_limit_bytes=16 * 1024 * 1024),
    )(live_counts, sums)


def solution(mesh):
    return jax.shard_map(
        functools.partial(per_device, mesh.shape["box"], mesh.shape["freq"]),
        mesh=mesh,
        in_specs=(
            P(("box", "freq"), None, None, None),
            P(("box", "freq"), None, None, None),
            P(None, None, None, None, "freq"),
            P("box", None),
            P("box", None),
            P("box", None),
        ),
        out_specs=(P("box", None, None, "freq"), P("box", None, None, "freq")),
        check_vma=False,
    )
```

time: 46.7 us -> 40.9 us (0.88)
  the two profiles are of different devices: /device:TPU:27 before, /device:TPU:1 now
where the time goes in v5:
time: 40.9 us; the launch traced here: 40.7 us
  Pallas kernels  39 us (95%)
  local copies, waits for them, and re-layouts  1.08 us (3%)
  between operations  0.66 us (2%)
    pallas_call x1, Pallas kernels, per_device(): pl.pallas_call(functools.partial(kernel, n_box, n_freq), out_shape=jax.Sh...  36.1 us
    pallas_call x1, Pallas kernels, per_device(): pl.pallas_call(unfold, out_shape=(jax.ShapeDtypeStruct((groups, 2, 8, LAN...  2.86 us
    unnamed x4, local copies, waits for them, and re-layouts  1.08 us

profile of v5, /device:TPU:1, one launch (start us, length us, event | category | flops | bytes accessed | tf_op | source)
XLA Modules:
  0.0 40.7 jit_solution(17779759925148563548)
XLA Ops:
  0.6 0.0 copy-start.1
  0.6 36.1 %shard_map.77.sums_ref = f32[16,80,128]{2,1,0:T(8,128)} custom-call(s32[1,2]{1,0:T(1,128)} %live_ref.3, bf16[8,2,8,1024]{3,2,1,0:T(8,128)(2,1)} %fine_ref.1, bf16[1,2,8,1024]{3,2,1,0:T(8,128)(2,1)} %coarse_ref.1, bf16[26,2,8,8,128]{4,3,2,1,0:T(8,128)(2,1)} %table_ref.1, s32[26,64]{1,0:T(8,128)} %bitcast.1, s32[8,26]{1,0:T(8,128)} %lists_coarse_ref.1), custom_call_target="tpu_custom_call" | custom-call | tf_op jit(solution)/shard_map/pallas_call | solution.py:458
  36.8 0.0 copy-done.1
  36.8 0.0 copy-start
  36.8 1.1 %copy-done = f32[16,80,128]{2,1,0:T(8,128)S(1)} copy-done((f32[16,80,128]{2,1,0:T(8,128)S(1)}, f32[16,80,128]{2,1,0:T(8,128)}, u32[]{:S(2)}) %copy-start) | copy-done | bytes 655384
  37.9 2.9 %shard_map.78 = (bf16[64,2,8,128]{3,2,1,0:T(8,128)(2,1)}, bf16[8,2,8,128]{3,2,1,0:T(8,128)(2,1)}) custom-call(s32[1,2]{1,0:T(1,128)S(1)} %copy-done.1, f32[16,80,128]{2,1,0:T(8,128)S(1)} %copy-done), custom_call_target="tpu_custom_call" | custom-call | tf_op jit(solution)/shard_map/pallas_call | solution.py:483
Async XLA Ops:
  0.6 36.1 %copy-start.1 = (s32[1,2]{1,0:T(1,128)S(1)}, s32[1,2]{1,0:T(1,128)}, u32[]{:S(2)}) copy-start(s32[1,2]{1,0:T(1,128)} %live_ref.3) | copy-start | bytes 28
  36.8 1.1 %copy-start = (f32[16,80,128]{2,1,0:T(8,128)S(1)}, f32[16,80,128]{2,1,0:T(8,128)}, u32[]{:S(2)}) copy-start(f32[16,80,128]{2,1,0:T(8,128)} %shard_map.77.sums_ref) | copy-start | bytes 1966084

commit v6 on v5

--- a/solution.py
+++ b/solution.py
@@ -65,12 +65,23 @@
     n_box,
     n_freq,
     live_ref,
+    fine_hbm,
+    coarse_hbm,
+    table_hbm,
+    lists_fine_hbm,
+    lists_coarse_hbm,
+    out_fine_hbm,
+    out_coarse_hbm,
+    out_fine_ref,
+    out_coarse_ref,
+    sums,
+    store_sem,
     fine_ref,
     coarse_ref,
     table_ref,
     lists_fine_ref,
     lists_coarse_ref,
-    sums,
+    load_sem,
     outbox,
     held,
     picks,
@@ -114,6 +125,21 @@
     def signal(semaphore, **device):
         pl.semaphore_signal(semaphore, inc=1, device_id=device)
 
+    loads = [
+        pltpu.make_async_copy(source, target, load_sem.at[i])
+        for i, (source, target) in enumerate(
+            (
+                (fine_hbm, fine_ref),
+                (coarse_hbm, coarse_ref),
+                (lists_fine_hbm, lists_fine_ref),
+                (lists_coarse_hbm, lists_coarse_ref),
+                (table_hbm, table_ref),
+            )
+        )
+    ]
+    for load in loads:
+        load.start()
+
     barrier = pltpu.get_barrier_semaphore()
     for near, other in ((near_above, above), (near_below, below)):
 
@@ -176,6 +202,8 @@
         outbox[j] = jnp.concatenate([both, *rows_of], axis=1)
         return carry
 
+    for load in loads[:2]:
+        load.wait()
     lax.fori_loop(0, n_freq, cut, 0, unroll=True)
 
     pl.semaphore_wait(barrier, ready)
@@ -285,6 +313,8 @@
             held[n_freq + 2 + i] = blank
 
     def prepare():
+        for load in loads[2:]:
+            load.wait()
         fine_list = jnp.transpose(lists_fine_ref[...])
         fine_at = fine_list - (box * groups - RIM_FINE)
         fine_row = jnp.where(fine_list >= 0, (fine_at // 8) * 16 + fine_at % 8, -1000)
@@ -327,7 +357,7 @@
         lax.fori_loop(0, slots // 2, widen, 0)
 
     def middle(turn, carry):
-        local = (turn == 0) == (early & (col < n_freq // 2))
+        local = (turn == 0) == (early & (col < 2))
 
         @pl.when(local)
         def _():
@@ -411,41 +441,59 @@
 
     lax.fori_loop(0, PAIRS, advance, 0)
 
-    for part in range(len(PARTS)):
-        for step in steps:
-            swap_copy(part, step).wait_send()
-        for up, near, gives in ((True, near_above, gives_above), (False, near_below, gives_below)):
-
-            @pl.when(near)
-            def _():
-                rim_copy(part, up).wait_send()
-
-            @pl.when(gives)
-            def _():
-                for copy in far_copies(up, part):
-                    copy.wait_send()
-
-
-def unfold(live_ref, sums_ref, out_fine_ref, out_coarse_ref):
-    groups = out_fine_ref.shape[0]
-    coarse_groups = out_coarse_ref.shape[0]
-
     def back(first, place, live, count, scale):
-        keep = alive(place + lax.broadcasted_iota(jnp.int32, (8, 8, LANES), 0), count, live)
-        planes = swap_blocks([sums_ref[b, pl.ds(first, 8)] for b in range(2 * BANDS)])
+        keep = alive(place + lax.broadcasted_iota(jnp.int32, (16, 8, LANES), 0), count, live)
+        planes = swap_blocks([sums[b, pl.ds(first, 16)] for b in range(2 * BANDS)])
         result = []
         for c in range(2):
             turned = jnp.swapaxes(jnp.stack(planes[8 * c : 8 * c + 8], axis=0), 0, 1)
             result.append(jnp.where(keep, scale * turned, 0.0).astype(jnp.bfloat16))
         return result
 
-    for first in range(0, groups, 8):
-        result = back(first, first, live_ref[0, 0], groups, 1.0)
+    stores = []
+    result = back(groups, 0, live_coarse, coarse_groups, 0.5)
+    for c in range(2):
+        out_coarse_ref[:, c] = result[c][:coarse_groups]
+    stores.append(pltpu.make_async_copy(out_coarse_ref, out_coarse_hbm, store_sem.at[0]))
+    stores[-1].start()
+    for first in range(0, groups, 16):
+        result = back(first, first, live_fine, groups, 1.0)
+        part = pl.ds(first, 16)
         for c in range(2):
-            out_fine_ref[pl.ds(first, 8), c] = result[c]
-    result = back(groups, 0, live_ref[0, 1], coarse_groups, 0.5)
-    for c in range(2):
-        out_coarse_ref[:, c] = result[c]
+            out_fine_ref[part, c] = result[c]
+        stores.append(
+            pltpu.make_async_copy(
+                out_fine_ref.at[part], out_fine_hbm.at[part], store_sem.at[first // 16 + 1]
+            )
+        )
+        stores[-1].start()
+    for store in stores:
+        store.wait()
+
+    for part in range(len(PARTS)):
+        for step in steps:
+            swap_copy(part, step).wait_send()
+        for up, near, gives in ((True, near_above, gives_above), (False, near_below, gives_below)):
+
+            @pl.when(near)
+            def _():
+                rim_copy(part, up).wait_send()
+
+            @pl.when(gives)
+            def _():
+                for copy in far_copies(up, part):
+                    copy.wait_send()
+
+
+def hand_over(fine_hbm, coarse_hbm, out_fine_hbm, out_coarse_hbm, fine_ref, coarse_ref, load_sem, store_sem):
+    moves = ((fine_hbm, fine_ref, out_fine_hbm), (coarse_hbm, coarse_ref, out_coarse_hbm))
+    for i, (source, held, _) in enumerate(moves):
+        pltpu.make_async_copy(source, held, load_sem.at[i]).start()
+    for i, (source, held, target) in enumerate(moves):
+        pltpu.make_async_copy(source, held, load_sem.at[i]).wait()
+        pltpu.make_async_copy(held, target, store_sem.at[i]).start()
+    for i, (_, held, target) in enumerate(moves):
+        pltpu.make_async_copy(held, target, store_sem.at[i]).wait()
 
 
 def per_device(n_box, n_freq, spectra_fine, spectra_coarse, kernel_table, lists_fine, lists_coarse, live_counts):
@@ -453,14 +501,29 @@
     coarse_groups = lists_coarse.shape[0]
     own = spectra_fine.shape[0]
     rows = groups + 16
-    vmem = pl.BlockSpec(memory_space=pltpu.VMEM)
+    hbm = pl.BlockSpec(memory_space=pltpu.HBM)
+    smem = pl.BlockSpec(memory_space=pltpu.SMEM)
     dma = pltpu.SemaphoreType.DMA
-    sums = pl.pallas_call(
+    results = (
+        jax.ShapeDtypeStruct((groups, 2, 8, LANES), jnp.bfloat16),
+        jax.ShapeDtypeStruct((coarse_groups, 2, 8, LANES), jnp.bfloat16),
+    )
+    result_scratch = [pltpu.VMEM(r.shape, r.dtype) for r in results]
+    fine, coarse = pl.pallas_call(
         functools.partial(kernel, n_box, n_freq),
-        out_shape=jax.ShapeDtypeStruct((2 * BANDS, rows, LANES), jnp.float32),
-        in_specs=[pl.BlockSpec(memory_space=pltpu.SMEM)] + [vmem] * 5,
-        out_specs=vmem,
-        scratch_shapes=[
+        out_shape=results,
+        in_specs=[smem] + [hbm] * 5,
+        out_specs=(hbm, hbm),
+        scratch_shapes=result_scratch
+        + [
+            pltpu.VMEM((2 * BANDS, rows, LANES), jnp.float32),
+            dma((groups // 16 + 1,)),
+            pltpu.VMEM(spectra_fine.shape, jnp.bfloat16),
+            pltpu.VMEM(spectra_coarse.shape, jnp.bfloat16),
+            pltpu.VMEM(kernel_table.shape, jnp.bfloat16),
+            pltpu.VMEM((slots, groups), jnp.int32),
+            pltpu.VMEM((coarse_groups, slots), jnp.int32),
+            dma((5,)),
             pltpu.VMEM((n_freq, 2 * own, PACK), jnp.bfloat16),
             pltpu.VMEM((16, 16, PACK), jnp.bfloat16),
             pltpu.VMEM((2, slots * rows, WIDE), jnp.bfloat16),
@@ -481,15 +544,13 @@
         ),
     )(live_counts, spectra_fine, spectra_coarse, kernel_table, lists_fine.T, lists_coarse)
     return pl.pallas_call(
-        unfold,
-        out_shape=(
-            jax.ShapeDtypeStruct((groups, 2, 8, LANES), jnp.bfloat16),
-            jax.ShapeDtypeStruct((coarse_groups, 2, 8, LANES), jnp.bfloat16),
-        ),
-        in_specs=[pl.BlockSpec(memory_space=pltpu.SMEM), vmem],
-        out_specs=(vmem, vmem),
-        compiler_params=pltpu.CompilerParams(vmem_limit_bytes=16 * 1024 * 1024),
-    )(live_counts, sums)
+        hand_over,
+        out_shape=results,
+        in_specs=[hbm, hbm],
+        out_specs=(hbm, hbm),
+        scratch_shapes=result_scratch + [dma((2,)), dma((2,))],
+        compiler_params=pltpu.CompilerParams(vmem_limit_bytes=60 * 1024 * 1024),
+    )(fine, coarse)
 
 
 def solution(mesh):

time: 40.9 us -> 39.2 us (0.958)
  local copies, waits for them, and re-layouts: 1.08 us -> 0 us
  Pallas kernels: 39 us -> 38.4 us
    unnamed x4 -> x0, local copies, waits for them, and re-layouts: 1.08 us -> none
    pallas_call x2, Pallas kernels: 39 us -> 38.4 us  [the longest x1 36.7 us: per_device(): pl.pallas_call(functools.partial(kernel, n_box, n_freq), out_shape=result...]
where the time goes in v6:
time: 39.2 us; the launch traced here: 39 us
  Pallas kernels  38.4 us (98%)
  between operations  0.64 us (2%)
    pallas_call x1, Pallas kernels, per_device(): pl.pallas_call(functools.partial(kernel, n_box, n_freq), out_shape=result...  36.7 us
    pallas_call x1, Pallas kernels, per_device(): pl.pallas_call(hand_over, out_shape=results, in_specs=[hbm, hbm], out_spe...  1.69 us

profile of v6, /device:TPU:1, one launch (start us, length us, event | category | flops | bytes accessed | tf_op | source)
XLA Modules:
  0.0 39.0 jit_solution(17971556713797652546)
XLA Ops:
  0.6 36.7 %shard_map.77 = (bf16[64,2,8,128]{3,2,1,0:T(8,128)(2,1)}, bf16[8,2,8,128]{3,2,1,0:T(8,128)(2,1)}) custom-call(s32[1,2]{1,0:T(1,128)} %live_ref.1, bf16[8,2,8,1024]{3,2,1,0:T(8,128)(2,1)} %fine_hbm.1, bf16[1,2,8,1024]{3,2,1,0:T(8,128)(2,1)} %coarse_hbm.1, bf16[26,2,8,8,128]{4,3,2,1,0:T(8,128)(2,1)} %table_hbm.1, s32[26,64]{1,0:T(8,128)} %bitcast.1, ...), custom_call_target="tpu_custom_call" | custom-call | tf_op jit(solution)/shard_map/pallas_call | solution.py:512
  37.4 1.7 %shard_map.78 = (bf16[64,2,8,128]{3,2,1,0:T(8,128)(2,1)}, bf16[8,2,8,128]{3,2,1,0:T(8,128)(2,1)}) custom-call(bf16[64,2,8,128]{3,2,1,0:T(8,128)(2,1)} %get-tuple-element.4.fine_hbm, bf16[8,2,8,128]{3,2,1,0:T(8,128)(2,1)} %get-tuple-element.5.coarse_hbm), custom_call_target="tpu_custom_call" | custom-call | tf_op jit(solution)/shard_map/pallas_call | solution.py:546

commit v7 on v6

--- a/solution.py
+++ b/solution.py
@@ -121,6 +121,7 @@
 
     early = lax.rem(box // HALF, 2) == 0
     late = jnp.logical_not(early)
+    rank = col
 
     def signal(semaphore, **device):
         pl.semaphore_signal(semaphore, inc=1, device_id=device)
@@ -149,7 +150,7 @@
 
     for step in steps:
 
-        @pl.when(late | (col + step < n_freq))
+        @pl.when(late | (rank + step < n_freq))
         def _():
             signal(barrier, freq=lax.rem(col + step, n_freq))
 
@@ -177,7 +178,7 @@
         + jnp.where(gives_below, n_freq, 0)
     )
     ready = (
-        jnp.where(early, col, late_ready)
+        jnp.where(early, rank, late_ready)
         + near_above.astype(jnp.int32)
         + near_below.astype(jnp.int32)
     )
@@ -210,9 +211,9 @@
 
     for step in steps:
 
-        @pl.when(early & (col >= step))
-        def _():
-            signal(ready_sem.at[step], freq=col - step)
+        @pl.when(early & (rank >= step))
+        def _():
+            signal(ready_sem.at[step], freq=lax.rem(col + n_freq - step, n_freq))
 
     for far, other, giver in ((far_above, above, 0), (far_below, below, n_freq - 2)):
 
@@ -276,16 +277,20 @@
 
     far_start(late)
     for part in range(len(PARTS)):
-        for step in order:
-
-            @pl.when(late | (col + step >= n_freq))
-            def _():
-                swap_copy(part, step).start()
+        for first_step, then_step in zip(steps, order):
+
+            @pl.when(early & (rank + first_step >= n_freq))
+            def _():
+                swap_copy(part, first_step).start()
+
+            @pl.when(late)
+            def _():
+                swap_copy(part, then_step).start()
 
     def send_on():
         for step in steps:
 
-            @pl.when(early & (col + step < n_freq))
+            @pl.when(early & (rank + step < n_freq))
             def _():
                 pl.semaphore_wait(ready_sem.at[step], 1)
                 for part in range(len(PARTS)):
@@ -357,7 +362,7 @@
         lax.fori_loop(0, slots // 2, widen, 0)
 
     def middle(turn, carry):
-        local = (turn == 0) == (early & (col < 2))
+        local = (turn == 0) == (early & (rank < 2))
 
         @pl.when(local)
         def _():

time: 39.2 us -> 37.2 us (0.949)
  the two profiles are of different devices: /device:TPU:1 before, /device:TPU:252 now
where the time goes in v7:
time: 37.2 us; the launch traced here: 37 us
  Pallas kernels  36.4 us (98%)
  between operations  0.64 us (2%)
    pallas_call x1, Pallas kernels, per_device(): pl.pallas_call(functools.partial(kernel, n_box, n_freq), out_shape=result...  34.7 us
    pallas_call x1, Pallas kernels, per_device(): pl.pallas_call(hand_over, out_shape=results, in_specs=[hbm, hbm], out_spe...  1.69 us

profile of v7, /device:TPU:252, one launch (start us, length us, event | category | flops | bytes accessed | tf_op | source)
XLA Modules:
  0.0 37.0 jit_solution(9366428325009235680)
XLA Ops:
  0.6 34.7 %shard_map.77 = (bf16[64,2,8,128]{3,2,1,0:T(8,128)(2,1)}, bf16[8,2,8,128]{3,2,1,0:T(8,128)(2,1)}) custom-call(s32[1,2]{1,0:T(1,128)} %live_ref.1, bf16[8,2,8,1024]{3,2,1,0:T(8,128)(2,1)} %fine_hbm.1, bf16[1,2,8,1024]{3,2,1,0:T(8,128)(2,1)} %coarse_hbm.1, bf16[26,2,8,8,128]{4,3,2,1,0:T(8,128)(2,1)} %table_hbm.1, s32[26,64]{1,0:T(8,128)} %bitcast.1, ...), custom_call_target="tpu_custom_call" | custom-call | tf_op jit(solution)/shard_map/pallas_call | solution.py:517
  35.3 1.7 %shard_map.78 = (bf16[64,2,8,128]{3,2,1,0:T(8,128)(2,1)}, bf16[8,2,8,128]{3,2,1,0:T(8,128)(2,1)}) custom-call(bf16[64,2,8,128]{3,2,1,0:T(8,128)(2,1)} %get-tuple-element.4.fine_hbm, bf16[8,2,8,128]{3,2,1,0:T(8,128)(2,1)} %get-tuple-element.5.coarse_hbm), custom_call_target="tpu_custom_call" | custom-call | tf_op jit(solution)/shard_map/pallas_call | solution.py:551

commit v8 on v7

--- a/solution.py
+++ b/solution.py
@@ -25,16 +25,15 @@
     count = len(planes)
     width = LANES // count
     block = lax.broadcasted_iota(jnp.int32, planes[0].shape, 1) // width
+    bits = [1 << i for i in range(count.bit_length() - 1)]
+    picked = {bit: (block & bit) != 0 for bit in bits}
     planes = list(planes)
-    step = count // 2
-    while step:
-        upper = (block & step) != 0
-        for p in range(count):
-            if p & step == 0:
-                first, second = planes[p], planes[p + step]
-                planes[p] = jnp.where(upper, pltpu.roll(second, width * step, 1), first)
-                planes[p + step] = jnp.where(upper, second, pltpu.roll(first, LANES - width * step, 1))
-        step //= 2
+    for bit in bits:
+        planes = [jnp.where(picked[bit], planes[(p + bit) % count], planes[p]) for p in range(count)]
+    planes = [planes[0]] + [pltpu.roll(planes[p], width * p, 1) for p in range(1, count)]
+    planes = [planes[-p % count] for p in range(count)]
+    for bit in bits:
+        planes = [jnp.where(picked[bit], planes[(p - bit) % count], planes[p]) for p in range(count)]
     return planes
 
 

time: 37.2 us -> 35.8 us (0.962)
  the two profiles are of different devices: /device:TPU:252 before, /device:TPU:1 now
where the time goes in v8:
time: 35.8 us; the launch traced here: 35.6 us
  Pallas kernels  35 us (98%)
  between operations  0.64 us (2%)
    pallas_call x1, Pallas kernels, per_device(): pl.pallas_call(functools.partial(kernel, n_box, n_freq), out_shape=result...  33.3 us
    pallas_call x1, Pallas kernels, per_device(): pl.pallas_call(hand_over, out_shape=results, in_specs=[hbm, hbm], out_spe...  1.69 us

profile of v8, /device:TPU:1, one launch (start us, length us, event | category | flops | bytes accessed | tf_op | source)
XLA Modules:
  0.0 35.6 jit_solution(16269346926422183947)
XLA Ops:
  0.6 33.3 %shard_map.77 = (bf16[64,2,8,128]{3,2,1,0:T(8,128)(2,1)}, bf16[8,2,8,128]{3,2,1,0:T(8,128)(2,1)}) custom-call(s32[1,2]{1,0:T(1,128)} %live_ref.1, bf16[8,2,8,1024]{3,2,1,0:T(8,128)(2,1)} %fine_hbm.1, bf16[1,2,8,1024]{3,2,1,0:T(8,128)(2,1)} %coarse_hbm.1, bf16[26,2,8,8,128]{4,3,2,1,0:T(8,128)(2,1)} %table_hbm.1, s32[26,64]{1,0:T(8,128)} %bitcast.1, ...), custom_call_target="tpu_custom_call" | custom-call | tf_op jit(solution)/shard_map/pallas_call | solution.py:516
  33.9 1.7 %shard_map.78 = (bf16[64,2,8,128]{3,2,1,0:T(8,128)(2,1)}, bf16[8,2,8,128]{3,2,1,0:T(8,128)(2,1)}) custom-call(bf16[64,2,8,128]{3,2,1,0:T(8,128)(2,1)} %get-tuple-element.4.fine_hbm, bf16[8,2,8,128]{3,2,1,0:T(8,128)(2,1)} %get-tuple-element.5.coarse_hbm), custom_call_target="tpu_custom_call" | custom-call | tf_op jit(solution)/shard_map/pallas_call | solution.py:550

commit v9 on v8

--- a/solution.py
+++ b/solution.py
@@ -108,7 +108,6 @@
     live_fine = live_ref[0, 0]
     live_coarse = live_ref[0, 1]
     steps = tuple(range(1, n_freq))
-    order = (4, 3, 5, 2, 6, 1, 7)
 
     has_above, has_below = box < n_box - 1, box > 0
     far_above = has_above & (lax.rem(box, HALF) == HALF - 1)
@@ -276,15 +275,18 @@
 
     far_start(late)
     for part in range(len(PARTS)):
-        for first_step, then_step in zip(steps, order):
-
-            @pl.when(early & (rank + first_step >= n_freq))
-            def _():
-                swap_copy(part, first_step).start()
-
-            @pl.when(late)
-            def _():
-                swap_copy(part, then_step).start()
+        for step in steps:
+
+            @pl.when(early & (rank + step >= n_freq))
+            def _():
+                swap_copy(part, step).start()
+
+        for peer in (4, 5, 6, 7, 3, 2, 1, 0):
+            step = lax.rem(peer + jnp.where(col < 4, 0, 4) + n_freq - col, n_freq)
+
+            @pl.when(late & (step > 0))
+            def _():
+                swap_copy(part, step).start()
 
     def send_on():
         for step in steps:

time: 35.8 us -> 35.8 us (level)
  no operation moved by 1% of the time
where the time goes in v9:
time: 35.8 us; the launch traced here: 35.6 us
  Pallas kernels  35 us (98%)
  between operations  0.64 us (2%)
    pallas_call x1, Pallas kernels, per_device(): pl.pallas_call(functools.partial(kernel, n_box, n_freq), out_shape=result...  33.3 us
    pallas_call x1, Pallas kernels, per_device(): pl.pallas_call(hand_over, out_shape=results, in_specs=[hbm, hbm], out_spe...  1.69 us

profile of v9, /device:TPU:1, one launch (start us, length us, event | category | flops | bytes accessed | tf_op | source)
XLA Modules:
  0.0 35.6 jit_solution(9978582258726744119)
XLA Ops:
  0.6 33.3 %shard_map.77 = (bf16[64,2,8,128]{3,2,1,0:T(8,128)(2,1)}, bf16[8,2,8,128]{3,2,1,0:T(8,128)(2,1)}) custom-call(s32[1,2]{1,0:T(1,128)} %live_ref.1, bf16[8,2,8,1024]{3,2,1,0:T(8,128)(2,1)} %fine_hbm.1, bf16[1,2,8,1024]{3,2,1,0:T(8,128)(2,1)} %coarse_hbm.1, bf16[26,2,8,8,128]{4,3,2,1,0:T(8,128)(2,1)} %table_hbm.1, s32[26,64]{1,0:T(8,128)} %bitcast.1, ...), custom_call_target="tpu_custom_call" | custom-call | tf_op jit(solution)/shard_map/pallas_call | solution.py:518
  33.9 1.7 %shard_map.78 = (bf16[64,2,8,128]{3,2,1,0:T(8,128)(2,1)}, bf16[8,2,8,128]{3,2,1,0:T(8,128)(2,1)}) custom-call(bf16[64,2,8,128]{3,2,1,0:T(8,128)(2,1)} %get-tuple-element.4.fine_hbm, bf16[8,2,8,128]{3,2,1,0:T(8,128)(2,1)} %get-tuple-element.5.coarse_hbm), custom_call_target="tpu_custom_call" | custom-call | tf_op jit(solution)/shard_map/pallas_call | solution.py:552
